TPU v7x, 128 devices: a whole 4x4x4 slice. The times are simulated.
128 devices in a mesh: dp: 16 (over x_hi, y, core), vocab: 8 (over z, x_lo).
Axes of the slice: x: 4 (x_hi: 2, x_lo: 2; x = x_hi * 2 + x_lo), y: 4, z: 4, core: 2. Of those that a mesh axis runs over, the one named last changes fastest.
Arguments:
- teacher_hidden: bfloat16 [768, 4608], P('dp', 'vocab'), may hold values from -6 to 6
- teacher_gain: bfloat16 [4608], P('vocab'), may hold values from 0.25 to 1.75
- teacher_head: bfloat16 [131072, 4608], P(('dp', 'vocab')), as said below
- student_hidden: bfloat16 [768, 3584], P('dp', 'vocab'), may hold values from -0.59765625 to 0.59765625
- student_gain: bfloat16 [3584], P('vocab'), may hold values from 0.25 to 1.75
- student_table: bfloat16 [131072, 3584], P(('dp', 'vocab')), as said below
- embed_cot: bfloat16 [768, 3584], P('dp', 'vocab'), may hold values from -0.011962891 to 0.011962891
- token_ids: int32 [768], P('dp'), may hold values from 0 to 131071
Outputs:
- hidden_grad: bfloat16 [768, 3584], P('dp', 'vocab')
- table_grad: bfloat16 [131072, 3584], P(('dp', 'vocab'))
Inputs may be any that keep to these rules, and one draw needn't show every extreme that they name: Each row of teacher_head and student_table is drawn independently. `student_table`: each row is drawn independently.
All inputs are finite; a program needn't handle non-finite values.
Results may differ from a plain program's by a relative error of at most 0.0087.
Values may be sent and summed in bfloat16 or wider, within the bound.
A program may use at most 192 MiB of HBM per device.

v0:
```python
import math

import jax
import jax.numpy as jnp
from jax import lax
from jax.sharding import PartitionSpec as P


def rms_norm(hidden, gain):
    values = hidden.astype(jnp.float32)
    scale = lax.rsqrt(jnp.mean(values * values, axis=1, keepdims=True) + 1e-06)
    return ((values * scale * gain.astype(jnp.float32)[None, :]).astype(jnp.bfloat16), scale)


def head_logits(normed, table):
    return lax.dot_general(
        normed, table, (((1,), (1,)), ((), ())), preferred_element_type=jnp.float32
    )


def per_device(
    teacher_hidden,
    teacher_gain,
    teacher_head,
    student_hidden,
    student_gain,
    student_table,
    embed_cot,
    token_ids,
):
    tok_dev = teacher_hidden.shape[0]
    block_width = student_hidden.shape[1]
    t_cols, t_gain, s_cols, s_gain, e_cols = (
        lax.all_gather(teacher_hidden, "vocab", axis=1, tiled=True),
        lax.all_gather(teacher_gain[None, :], "vocab", axis=1, tiled=True),
        lax.all_gather(student_hidden, "vocab", axis=1, tiled=True),
        lax.all_gather(student_gain[None, :], "vocab", axis=1, tiled=True),
        lax.all_gather(embed_cot, "vocab", axis=1, tiled=True),
    )
    t_full, s_full, e_full = (
        lax.all_gather(t_cols, "dp", axis=0, tiled=True),
        lax.all_gather(s_cols, "dp", axis=0, tiled=True),
        lax.all_gather(e_cols, "dp", axis=0, tiled=True),
    )
    ids_full = lax.all_gather(token_ids, "dp", axis=0, tiled=True)
    full_width = s_full.shape[1]
    t_normed, t_scale = rms_norm(t_full, t_gain[0])
    s_normed, s_scale_full = rms_norm(s_full, s_gain[0])
    t_exp = jnp.exp(30.0 * jnp.tanh(head_logits(t_normed, teacher_head) / 30.0))
    s_raw = head_logits(s_normed, student_table)
    s_tanh = jnp.tanh(s_raw / 30.0)
    s_exp = jnp.exp(30.0 * s_tanh)
    t_total, s_total = lax.psum((jnp.sum(t_exp, axis=1), jnp.sum(s_exp, axis=1)), ("dp", "vocab"))
    logit_grad = (
        (s_exp / s_total[:, None] - t_exp / t_total[:, None]) * (1.0 - s_tanh * s_tanh)
    ).astype(jnp.bfloat16)
    tok_start = lax.axis_index("dp") * tok_dev
    col_start = lax.axis_index("vocab") * block_width
    summed = lax.psum(
        jnp.dot(logit_grad, student_table, preferred_element_type=jnp.float32), ("dp", "vocab")
    )
    normed_grad = lax.dynamic_slice(summed, (tok_start, col_start), (tok_dev, block_width))
    s_scale = lax.dynamic_slice_in_dim(s_scale_full, tok_start, tok_dev, 0)
    normed_block = lax.dynamic_slice(
        s_normed, (tok_start, col_start), (tok_dev, block_width)
    ).astype(jnp.float32)
    inner = lax.psum(jnp.sum(normed_grad * normed_block, axis=1), "vocab")[:, None]
    hidden_grad = s_scale * student_gain.astype(jnp.float32)[None, :] * normed_grad
    hidden_grad = (
        hidden_grad - student_hidden.astype(jnp.float32) * s_scale * s_scale * inner / full_width
    )
    vocab_rows = student_table.shape[0]
    table_grad = lax.dot_general(
        logit_grad, s_normed, (((0,), (0,)), ((), ())), preferred_element_type=jnp.float32
    )
    local_ids = ids_full - lax.axis_index(("dp", "vocab")) * vocab_rows
    inside = (local_ids >= 0) & (local_ids < vocab_rows)
    local_ids = jnp.where(inside, local_ids, vocab_rows)
    embed_rows = jax.ops.segment_sum(
        e_full.astype(jnp.float32) * math.sqrt(full_width), local_ids, num_segments=vocab_rows + 1
    )
    table_grad = table_grad + embed_rows[:vocab_rows]
    return (hidden_grad.astype(jnp.bfloat16), table_grad.astype(jnp.bfloat16))


def solution(mesh):
    return jax.shard_map(
        per_device,
        mesh=mesh,
        in_specs=(
            P("dp", "vocab"),
            P("vocab"),
            P(("dp", "vocab"), None),
            P("dp", "vocab"),
            P("vocab"),
            P(("dp", "vocab"), None),
            P("dp", "vocab"),
            P("dp"),
        ),
        out_specs=(P("dp", "vocab"), P(("dp", "vocab"), None)),
        check_vma=False,
    )
```

profile of v0, /device:TPU:0, one launch (start us, length us, event | category | flops | bytes accessed | tf_op | source)
XLA Modules:
  0.0 463.1 jit_solution(1520306974452411598)
XLA Ops:
  7.2 31.0 %all-gather.2 = bf16[8,448,48]{1,2,0:T(8,128)(2,1)S(1)} all-gather(bf16[1,448,48]{1,2,0:T(8,128)(2,1)} %bitcast.29), channel_id=1, replica_groups=mesh['dp'=16,'vocab'=8] {'vocab'}, dimensions={0}, use_global_device_ids=true | all-gather | bytes 387072 | tf_op jit(solution)/shard_map/all_gather | solution.py:36
  38.5 1.1 reshape.66
  39.7 31.3 %all-gather.3 = bf16[8,576,48]{1,2,0:T(8,128)(2,1)S(1)} all-gather(bf16[1,576,48]{1,2,0:T(8,128)(2,1)} %bitcast.30), channel_id=1, replica_groups=mesh['dp'=16,'vocab'=8] {'vocab'}, dimensions={0}, use_global_device_ids=true | all-gather | bytes 497664 | tf_op jit(solution)/shard_map/all_gather | solution.py:34
  71.1 1.1 reshape.68
  72.3 30.7 %all-gather.4 = bf16[8,448,48]{1,2,0:T(8,128)(2,1)S(1)} all-gather(bf16[1,448,48]{1,2,0:T(8,128)(2,1)} %bitcast.31), channel_id=1, replica_groups=mesh['dp'=16,'vocab'=8] {'vocab'}, dimensions={0}, use_global_device_ids=true | all-gather | bytes 387072 | tf_op jit(solution)/shard_map/all_gather | solution.py:38
  103.2 1.2 reshape.70
  106.8 34.6 %all-reduce.4 = (bf16[3584]{0:T(1024)(128)(2,1)S(1)}, bf16[4608]{0:T(1024)(128)(2,1)S(1)}) all-reduce(bf16[3584]{0:T(1024)(128)(2,1)S(1)} %dynamic-update-slice, bf16[4608]{0:T(1024)(128)(2,1)S(1)} %dynamic-update-slice.1), channel_id=2, replica_groups=mesh['dp'=16,'vocab'=8] {'vocab'}, use_global_device_ids=true, to_apply=%add | all-reduce | flops 8192 | bytes 32768
  141.5 3.9 fusion.4
  145.7 2.2 fusion.6
  147.9 2.5 copy-done.2
  150.3 7.7 %fusion.16 = (f32[768]{0:T(1024)S(1)}, f32[768,1024]{1,0:T(8,128)}) fusion(bf16[768,3584]{1,0:T(8,128)(2,1)S(1)} %fusion.6, bf16[1024,3584]{1,0:T(8,128)(2,1)S(1)} %copy-done.6), kind=kOutput, calls=%fused_computation.24 | convolution fusion | flops 5639502848 | bytes 15993856 | tf_op jit(solution)/shard_map/dot_general | solution.py:16
  158.0 15.9 %all-gather.11.cloned.1.call-done = bf16[768,4608]{1,0:T(8,128)(2,1)} async-done(((bf16[48,4608]{1,0:T(8,128)(2,1)}), bf16[768,4608]{1,0:T(8,128)(2,1)}) %all-gather.11.cloned.1.call-update) | async-done | bytes 7077904 | tf_op jit(solution)/shard_map/all_gather | solution.py:41
  173.9 4.6 fusion.1
  178.9 11.7 %fusion.17 = (f32[768]{0:T(1024)S(1)}, f32[768,1024]{1,0:T(8,128)}) fusion(bf16[1024,4608]{1,0:T(8,128)(2,1)} %param.10, bf16[768,4608]{1,0:T(8,128)(2,1)S(1)} %copy-done.1, f32[4608]{0:T(1024)S(1)} %mul.153, f32[768]{0:T(1024)S(1)} %add_rsqrt_fusion), kind=kOutput, calls=%fused_computation.26 | convolution fusion | flops 7264271360 | bytes 19685376 | tf_op jit(solution)/shard_map/dot_general | solution.py:16
  190.6 67.6 %all-reduce.3 = (f32[768]{0:T(1024)S(1)}, f32[768]{0:T(1024)S(1)}) all-reduce(f32[768]{0:T(1024)S(1)} %get-tuple-element.6, f32[768]{0:T(1024)S(1)} %get-tuple-element.8), channel_id=1, replica_groups=mesh['dp'=16,'vocab'=8] {'dp','vocab'}, use_global_device_ids=true, to_apply=%region_5.0 | all-reduce | flops 1536 | bytes 12288 | tf_op jit(solution)/shard_map/psum | solution.py:53
  258.2 13.7 %fusion.18 = f32[768,3584]{1,0:T(8,128)} fusion(bf16[1024,3584]{1,0:T(8,128)(2,1)} %param.13, f32[768,1024]{1,0:T(8,128)} %get-tuple-element.9, f32[768,1024]{1,0:T(8,128)} %get-tuple-element.7, f32[768]{0:T(1024)S(1)} %get-tuple-element.2, f32[768]{0:T(1024)S(1)} %get-tuple-element.3), kind=kOutput, calls=%fused_computation.32 | convolution fusion | flops 5645795328 | bytes 24647680 | tf_op jit(solution)/shard_map/dot_general | solution.py:60
  272.0 0.6 copy-done.8
  274.1 11.8 %all-reduce.2 = s32[768]{0:T(1024)S(1)} all-reduce(s32[768]{0:T(1024)S(1)} %dynamic-update-slice.2), channel_id=1, replica_groups=mesh['dp'=16,'vocab'=8] {'dp'}, use_global_device_ids=true, to_apply=%add.2 | all-reduce | flops 768 | bytes 6144
  286.0 28.4 %scatter_custom_fusion = f32[1025,3584]{1,0:T(8,128)} fusion(s32[768]{0:T(1024)S(1)} %and_select_fusion, bf16[768,3584]{1,0:T(8,128)(2,1)} %all-gather.13.cloned.1.call-done, f32[]{:T(128)} %constant.18.clone.1, f32[]{:T(128)} %constant.46.clone.1), kind=kCustom, calls=%fused_computation.13 | custom fusion | flops 8257536 | bytes 20199432 | tf_op jit(solution)/shard_map/scatter-add | solution.py:79
  314.4 14.5 %fusion = bf16[1024,3584]{1,0:T(8,128)(2,1)} fusion(f32[1025,3584]{1,0:T(8,128)} %scatter_custom_fusion, bf16[768,3584]{1,0:T(8,128)(2,1)} %copy-done.2, f32[768,1024]{1,0:T(8,128)S(1)} %copy-done.10, f32[768,1024]{1,0:T(8,128)} %get-tuple-element.7, f32[768]{0:T(1024)S(1)} %get-tuple-element.2, f32[768]{0:T(1024)S(1)} %get-tuple-element.3), kind=kOutput, calls=%fused_computation.4 | convolution fusion | flops 5653135360 | bytes 33822720 | tf_op jit(solution)/shard_map/dot_general | solution.py:73
  328.9 107.1 %all-reduce.7.cloned.1.call-done = f32[768,3584]{1,0:T(8,128)} async-done(((f32[768,3584]{1,0:T(8,128)}), f32[768,3584]{1,0:T(8,128)}) %all-reduce.7.cloned.1.call-update) | async-done | bytes 11010064 | tf_op jit(solution)/shard_map/psum | solution.py:59
  436.0 1.1 multiply_reduce_fusion
  437.1 17.8 %psum.31 = f32[48]{0:T(128)S(1)} all-reduce(f32[48]{0:T(128)S(1)} %multiply_reduce_fusion), channel_id=1, replica_groups=mesh['dp'=16,'vocab'=8] {'vocab'}, use_global_device_ids=true, to_apply=%region_8.0 | all-reduce | flops 48 | bytes 384 | tf_op jit(solution)/shard_map/psum | solution.py:67
  454.9 1.6 subtract_convert_fusion
  (48 shorter events, 3.6 us)
Async XLA Ops:
  7.2 97.3 %copy-start.9 = (u32[128]{0:T(128)S(1)}, u32[128]{0:T(128)}, u32[]{:S(2)}) copy-start(u32[128]{0:T(128)} %constant.49) | copy-start | bytes 1540
  7.2 99.2 %copy-start.5 = (bf16[576]{0:T(1024)(128)(2,1)S(1)}, bf16[576]{0:T(1024)(128)(2,1)}, u32[]{:S(2)}) copy-start(bf16[576]{0:T(1024)(128)(2,1)} %param.9) | copy-start | bytes 3460
  7.2 99.4 %copy-start.4 = (bf16[448]{0:T(512)(128)(2,1)S(1)}, bf16[448]{0:T(512)(128)(2,1)}, u32[]{:S(2)}) copy-start(bf16[448]{0:T(512)(128)(2,1)} %param.12) | copy-start | bytes 2692
  7.2 134.3 %all-gather.9.cloned.1.call-start = ((), (), s32[]{:S(2)}) async-start(), calls=%async_computation | async-start | bytes 5849088 | tf_op jit(solution)/shard_map/all_gather | solution.py:42
  39.6 134.3 %all-gather.11.cloned.1.call-start = ((), (), s32[]{:S(2)}) async-start(), calls=%async_computation.1 | async-start | bytes 7520256 | tf_op jit(solution)/shard_map/all_gather | solution.py:41
  72.2 213.8 %all-gather.13.cloned.1.call-start = ((), (), s32[]{:S(2)}) async-start(), calls=%async_computation.3 | async-start | bytes 5849088 | tf_op jit(solution)/shard_map/all_gather | solution.py:43
  104.4 331.6 %all-reduce.7.cloned.1.call-start = ((), (), s32[]{:S(2)}) async-start(), calls=%async_computation.2 | async-start | bytes 22020096 | tf_op jit(solution)/shard_map/psum | solution.py:59
  141.5 4.2 copy-start
  145.7 4.7 %copy-start.6 = (bf16[1024,3584]{1,0:T(8,128)(2,1)S(1)}, bf16[1024,3584]{1,0:T(8,128)(2,1)}, u32[]{:S(2)}) copy-start(bf16[1024,3584]{1,0:T(8,128)(2,1)} %param.13) | copy-start | bytes 22020100
  147.9 2.5 copy-start.2
  173.9 5.0 %copy-start.1 = (bf16[768,4608]{1,0:T(8,128)(2,1)S(1)}, bf16[768,4608]{1,0:T(8,128)(2,1)}, u32[]{:S(2)}) copy-start(bf16[768,4608]{1,0:T(8,128)(2,1)} %all-gather.11.cloned.1.call-done) | copy-start | bytes 21233668
  271.9 0.7 copy-start.8
  271.9 1.9 copy-start.7
  286.0 28.4 %copy-start.10 = (f32[768,1024]{1,0:T(8,128)S(1)}, f32[768,1024]{1,0:T(8,128)}, u32[]{:S(2)}) copy-start(f32[768,1024]{1,0:T(8,128)} %get-tuple-element.9) | copy-start | bytes 9437188
  314.4 140.5 %copy-start.3 = (bf16[48,448]{1,0:T(8,128)(2,1)S(1)}, bf16[48,448]{1,0:T(8,128)(2,1)}, u32[]{:S(2)}) copy-start(bf16[48,448]{1,0:T(8,128)(2,1)} %param.11) | copy-start | bytes 129028
Sparse Core Ops, SparseCore 0:
  39.7 66.8 all-gather.8
  109.1 64.7 all-gather.10
  176.4 58.9 all-gather.12
  272.1 163.8 all-reduce.6
where the time goes:
time: 464 us; the launch traced here: 463 us
  blocking collectives  225 us (48%)
  waiting for transfers between devices  123 us (27%)
  matrix products  47.6 us (10%)
  other arithmetic  41.8 us (9%)
  between operations  15.9 us (3%)
  local copies, waits for them, and re-layouts  9.74 us (2%)
    psum x1, waiting for transfers between devices, per_device(): lax.psum(jnp.dot(logit_grad, student_table, preferred_element_type=jnp.fl...  107 us
    psum x1, blocking collectives, per_device(): lax.psum((jnp.sum(t_exp, axis=1), jnp.sum(s_exp, axis=1)), ('dp', 'vocab'))  67.6 us
    unnamed x2, blocking collectives  46.4 us
    all_gather x1, blocking collectives, per_device(): lax.all_gather(teacher_hidden, 'vocab', axis=1, tiled=True)  31.3 us
    all_gather x1, blocking collectives, per_device(): lax.all_gather(student_hidden, 'vocab', axis=1, tiled=True)  31 us
    all_gather x1, blocking collectives, per_device(): lax.all_gather(embed_cot, 'vocab', axis=1, tiled=True)  30.7 us
    scatter-add x1, other arithmetic, per_device(): jax.ops.segment_sum(e_full.astype(jnp.float32) * math.sqrt(full_width), l...  28.4 us
    dot_general x2, matrix products, head_logits(): lax.dot_general(normed, table, (((1,), (1,)), ((), ())), preferred_elemen...  19.4 us
  transfers between devices with their start and end apart: 4, of which 2 were waited for; matrix products, arithmetic and copies ran while one was open for 20% of the time, Pallas kernels for 0%

commit v1 on v0

v1 whole, which is shorter than its diff:
```python
import math

import jax
import jax.numpy as jnp
from jax import lax
from jax.experimental import pallas as pl
from jax.experimental.pallas import tpu as pltpu
from jax.sharding import PartitionSpec as P

MESH = pl.DeviceIdType.MESH
F32, BF16 = jnp.float32, jnp.bfloat16
ORDER = (("z", "x", "y"), ("x", "y", "z"), ("y", "z", "x"))
NT = (((1,), (1,)), ((), ()))
NN = (((1,), (0,)), ((), ()))


def dot(a, b, dims=NN):
    return lax.dot_general(a, b, dims, preferred_element_type=F32)


class Place:
    def __init__(self):
        dp, vocab = lax.axis_index("dp"), lax.axis_index("vocab")
        self.vocab, self.dp = vocab, dp
        self.core = dp % 2
        self.at = {"x": (dp // 8) * 2 + vocab % 2, "y": (dp // 2) % 4, "z": vocab // 2}
        self.x_lo = vocab % 2

    def device(self, core=None, **moved):
        at = {**self.at, **moved}
        core = self.core if core is None else core
        return ((at["x"] // 2) * 8 + at["y"] * 2 + core, at["z"] * 2 + at["x"] % 2)

    def along(self, axis, by):
        return (self.at[axis] + by) % 4

    def shifted(self, axis, by):
        return self.device(**{axis: self.along(axis, by)})

    def sibling(self):
        return self.device(core=1 - self.core)


class Copies:
    def __init__(self, send_sems, recv_sems):
        self.send_sems, self.recv_sems, self.count, self.all = send_sems, recv_sems, 0, []

    def start(self, src, dst, device):
        copy = pltpu.make_async_remote_copy(
            src_ref=src,
            dst_ref=dst,
            send_sem=self.send_sems.at[self.count],
            recv_sem=self.recv_sems.at[self.count],
            device_id=device,
            device_id_type=MESH,
        )
        self.count += 1
        copy.start()
        self.all.append(copy)
        return copy


def region(fixed, core, part, lanes):
    whole = slice(None)
    z, y = fixed.get("z", whole), fixed.get("y", whole)
    x_lo, x_hi = (fixed["x"] % 2, fixed["x"] // 2) if "x" in fixed else (whole, whole)
    return (z, x_lo, x_hi, y, core, pl.ds(16 * part, 16), lanes)


def gather(here, copies, buf, width):
    low, high, full = pl.ds(0, width // 2), pl.ds(width // 2, width // 2), pl.ds(0, width)
    to_sibling = []

    def slab(p, ph, by, lanes, core=None):
        axis = ORDER[p][ph]
        fixed = {a: here.at[a] for a in "xyz" if a not in ORDER[p][:ph]}
        fixed[axis] = here.along(axis, by)
        return buf.at[region(fixed, here.core if core is None else core, p, lanes)]

    def push(p, ph, by, lanes, device):
        piece = slab(p, ph, by, lanes)
        return copies.start(piece, piece, device)

    for ph in range(3):
        first = []
        for p in range(3):
            axis = ORDER[p][ph]
            first.append(
                (push(p, ph, 0, full, here.shifted(axis, 1)), push(p, ph, 0, full, here.shifted(axis, -1)))
            )
        if ph == 2:
            to_sibling += [push(p, ph, 0, full, here.sibling()) for p in range(3)]
        yield
        second = []
        for p in range(3):
            axis = ORDER[p][ph]
            first[p][0].wait_recv()
            right = push(p, ph, -1, low, here.shifted(axis, 1))
            first[p][1].wait_recv()
            left = push(p, ph, 1, high, here.shifted(axis, -1))
            second.append((right, left))
        if ph == 2:
            to_sibling += [push(p, ph, by, full, here.sibling()) for p in range(3) for by in (-1, 1)]
        yield
        for p in range(3):
            for copy in second[p]:
                copy.wait_recv()
            if ph == 2:
                to_sibling.append(push(p, ph, 2, full, here.sibling()))
    yield
    for copy in to_sibling:
        copy.wait_recv()


def scatter(here, copies, buf, halves, wholes, result):
    low, high, full = pl.ds(0, 256), pl.ds(256, 256), pl.ds(0, 512)

    def slab(p, ph, by, lanes):
        order = ORDER[p][::-1]
        fixed = {a: here.at[a] for a in order[:ph]}
        fixed[order[ph]] = here.along(order[ph], by)
        return region(fixed, here.core, p, lanes)

    for ph in range(3):
        first = []
        for p in range(3):
            axis = ORDER[p][2 - ph]
            got = halves[p * 3 + ph]
            first.append(
                (
                    copies.start(buf.at[slab(p, ph, 2, low)], got.at[0], here.shifted(axis, 1)),
                    copies.start(buf.at[slab(p, ph, 2, high)], got.at[1], here.shifted(axis, -1)),
                )
            )
        yield
        second = []
        for p in range(3):
            axis = ORDER[p][2 - ph]
            got, into = halves[p * 3 + ph], wholes[p * 3 + ph]
            first[p][0].wait_recv()
            at = slab(p, ph, 1, low)
            buf[at] = (buf[at].astype(F32) + got[0].astype(F32)).astype(BF16)
            right = copies.start(buf.at[slab(p, ph, 1, full)], into.at[0], here.shifted(axis, 1))
            first[p][1].wait_recv()
            at = slab(p, ph, -1, high)
            buf[at] = (buf[at].astype(F32) + got[1].astype(F32)).astype(BF16)
            left = copies.start(buf.at[slab(p, ph, -1, full)], into.at[1], here.shifted(axis, -1))
            second.append((right, left))
        yield
        for p in range(3):
            into = wholes[p * 3 + ph]
            for copy in second[p]:
                copy.wait_recv()
            at = slab(p, ph, 0, full)
            total = buf[at].astype(F32) + into[0].astype(F32) + into[1].astype(F32)
            if ph < 2:
                buf[at] = total.astype(BF16)
            else:
                result[pl.ds(16 * p, 16), :] = total
    yield


def scatter_shapes():
    sizes = {"x": (2, 2), "y": (4,), "z": (4,)}
    halves, wholes = [], []
    for order in ORDER:
        left = ["x", "y", "z"]
        for axis in order[::-1]:
            left.remove(axis)
            dims = sum((sizes[a] for a in ("z", "x", "y") if a in left), ())
            halves.append(pltpu.VMEM((2, *dims, 16, 256), BF16))
            wholes.append(pltpu.VMEM((2, *dims, 16, 512), BF16))
    return halves, wholes


def column_to_row(column):
    rows, lanes = lax.broadcasted_iota(jnp.int32, (48, 128), 0), lax.broadcasted_iota(jnp.int32, (48, 128), 1)
    return jnp.sum(jnp.where(rows == lanes, column, 0.0), axis=0, keepdims=True)


def row_to_column(row):
    rows, lanes = lax.broadcasted_iota(jnp.int32, (48, 128), 0), lax.broadcasted_iota(jnp.int32, (48, 128), 1)
    return jnp.sum(jnp.where(rows == lanes, row, 0.0), axis=1, keepdims=True)


def vocab_start(here, copies, slots, first_row, second_row):
    rows = lax.broadcasted_iota(jnp.int32, (8, 128), 0)
    slots[here.vocab] = jnp.where(rows == 0, first_row, jnp.where(rows == 1, second_row, 0.0))
    mine = slots.at[here.vocab]
    return [copies.start(mine, mine, (here.dp, (here.vocab + by) % 8)) for by in range(1, 8)]


def vocab_sum(slots, started):
    for copy in started:
        copy.wait_recv()
    total = slots[0]
    for slot in range(1, 8):
        total = total + slots[slot]
    return total


def kernel(
    th_ref, tgain_ref, head_hbm, sh_ref, sgain_ref, table_hbm, ec_ref, ids_ref,
    hidden_grad_ref, table_grad_hbm,
    A, E, R, SB, HEAD, ST, EXPT, STANH, LGT, LG, OHT, GR, MSG, GOT, SQ, INNER, SCALE, TS, TR,
    *rest,
):
    halves, wholes, (send_sems, recv_sems, sib_send, sib_recv, load_sems, out_sems) = rest[:9], rest[9:18], rest[18:]
    here = Place()
    copies = Copies(send_sems, recv_sems)
    x_lo = here.x_lo
    width = 3584

    barrier = pltpu.get_barrier_semaphore()
    partners = [here.shifted(axis, by) for axis in "xyz" for by in (1, 2, 3)] + [here.sibling()]
    partners += [(here.dp, here.along("z", by) * 2 + 1 - x_lo) for by in (1, 2, 3)]
    for partner in partners:
        pl.semaphore_signal(barrier, inc=1, device_id=partner, device_id_type=MESH)

    load_head = pltpu.make_async_copy(head_hbm, HEAD, load_sems.at[0])
    load_table = pltpu.make_async_copy(table_hbm, ST, load_sems.at[1])
    load_head.start()
    load_table.start()

    th, sh, ec = th_ref[...].astype(F32), sh_ref[...].astype(F32), ec_ref[...].astype(F32)
    tgain, sgain = tgain_ref[...].astype(F32), sgain_ref[...].astype(F32)
    low = x_lo == 0
    MSG[0:48, :] = jnp.concatenate([jnp.where(low, sh, th[:, :448]), ec[:, :64]], axis=1).astype(BF16)
    gain_row = jnp.concatenate([jnp.where(low, sgain, tgain[:, :448]), jnp.zeros((1, 64), F32)], axis=1)
    MSG[48:64, :] = jnp.broadcast_to(gain_row, (16, 512)).astype(BF16)
    t_part = jnp.sum(th * th, axis=1, keepdims=True)
    s_part = jnp.sum(sh * sh, axis=1, keepdims=True)
    pl.semaphore_wait(barrier, len(partners))
    pair = copies.start(MSG, GOT, (here.dp, here.vocab + 1 - 2 * x_lo))
    started = vocab_start(here, copies, SQ, column_to_row(t_part), column_to_row(s_part))
    sums = vocab_sum(SQ, started)
    t_scale = lax.rsqrt(row_to_column(sums[0:1]) / 4608 + 1e-06)
    s_scale = lax.rsqrt(row_to_column(sums[1:2]) / width + 1e-06)
    SCALE[...] = jnp.broadcast_to(s_scale, (48, 128))
    pair.wait_recv()
    got = GOT[0:48, :].astype(F32)
    got_gain = GOT[48:64, :].astype(F32)[0:1]

    values = jnp.where(
        low,
        jnp.concatenate([th, got[:, :448]], axis=1),
        jnp.concatenate([th[:, 448:], got[:, :448], sh], axis=1),
    )
    gains = jnp.where(
        low,
        jnp.concatenate([tgain, got_gain[:, :448]], axis=1),
        jnp.concatenate([tgain[:, 448:], got_gain[:, :448], sgain], axis=1),
    )
    lanes = lax.broadcasted_iota(jnp.int32, (48, 1024), 1)
    scales = jnp.where(jnp.logical_or(low, lanes < 128), t_scale, s_scale)
    own = (here.at["z"], x_lo, here.at["x"] // 2, here.at["y"], here.core)
    A[own] = (values * scales * gains).astype(BF16)

    ids = ids_ref[...]
    spot = lax.broadcasted_iota(jnp.int32, (48, 128), 1)
    digits = jnp.where(
        spot == 0, ids // 4096, jnp.where(spot == 1, (ids // 64) % 64, jnp.where(spot == 2, ids % 64, 0))
    ).astype(F32)
    E[own] = jnp.where(
        low,
        jnp.concatenate([ec, got[:, 448:]], axis=1),
        jnp.concatenate([ec[:, 64:], digits], axis=1),
    ).astype(BF16)

    for _ in gather(here, copies, A, 1024):
        pass
    cotangents = gather(here, copies, E, 512)
    next(cotangents)

    def t_step(m, total):
        rows = pl.ds(pl.multiple_of(m * 256, 256), 256)
        raw = jnp.zeros((256, 768), F32)
        for z in range(4):
            at = z * 1152
            raw += dot(HEAD[rows, at : at + 1024], A[z, 0].reshape(768, 1024), NT)
            raw += dot(HEAD[rows, at + 1024 : at + 1152], A[z, 1, :, :, :, :, 0:128].reshape(768, 128), NT)
        value = jnp.exp(30.0 * jnp.tanh(raw * (1.0 / 30.0)))
        EXPT[rows, :] = value
        return total + jnp.sum(value, axis=0, keepdims=True)

    def s_step(m, total):
        rows = pl.ds(pl.multiple_of(m * 256, 256), 256)
        raw = jnp.zeros((256, 768), F32)
        for z in range(4):
            raw += dot(
                ST[rows, z * 896 : z * 896 + 896], A[z, 1, :, :, :, :, 128:1024].reshape(768, 896), NT
            )
        value = jnp.tanh(raw * (1.0 / 30.0))
        STANH[rows, :] = value
        return total + jnp.sum(jnp.exp(30.0 * value), axis=0, keepdims=True)

    load_head.wait()
    t_total = lax.fori_loop(0, 2, t_step, jnp.zeros((1, 768), F32))
    next(cotangents)
    t_total = lax.fori_loop(2, 4, t_step, t_total)
    next(cotangents)
    load_table.wait()
    s_total = lax.fori_loop(0, 2, s_step, jnp.zeros((1, 768), F32))
    next(cotangents)
    s_total = lax.fori_loop(2, 4, s_step, s_total)

    rows = lax.broadcasted_iota(jnp.int32, (8, 768), 0)
    TS[0] = jnp.where(rows == 0, t_total, s_total)
    slot = 0
    for step, axis in enumerate(("core", "x", "y", "z")):
        if axis == "core":
            targets = [here.sibling()]
        else:
            targets = [here.shifted(axis, by) for by in (1, 2, 3)]
        sent = [copies.start(TS.at[step], TR.at[slot + i], target) for i, target in enumerate(targets)]
        total = TS[step]
        for i, copy in enumerate(sent):
            copy.wait_recv()
            total = total + TR[slot + i]
        slot += len(targets)
        TS[step + 1] = total
    next(cotangents)
    inverse = 1.0 / TS[4]
    t_inverse, s_inverse = inverse[0:1], inverse[1:2]

    def grad_step(m, carry):
        rows = pl.ds(pl.multiple_of(m * 256, 256), 256)
        tanh = STANH[rows, :]
        grad = (jnp.exp(30.0 * tanh) * s_inverse - EXPT[rows, :] * t_inverse) * (1.0 - tanh * tanh)
        LGT[rows, :] = grad.astype(BF16)
        LG[:, rows] = grad.T.astype(BF16)
        return carry

    lax.fori_loop(0, 4, grad_step, 0)

    def to_sibling(z, x):
        return pltpu.make_async_remote_copy(
            src_ref=R.at[z, x, :, :, 1 - here.core],
            dst_ref=SB.at[z, x],
            send_sem=sib_send.at[z * 2 + x],
            recv_sem=sib_recv.at[z * 2 + x],
            device_id=here.sibling(),
            device_id_type=MESH,
        )

    def normed_grad_step(z, carry):
        for x in range(2):
            for half in range(2):
                columns = pl.ds(pl.multiple_of(z * 896 + x * 384 + half * 256, 128), 256)
                block = dot(LG[...], ST[:, columns]).astype(BF16)
                R[z, x, :, :, :, :, half * 256 : half * 256 + 256] = block.reshape(2, 4, 2, 48, 256)
            to_sibling(z, x).start()
        return carry

    lax.fori_loop(0, 2, normed_grad_step, 0)
    next(cotangents)
    lax.fori_loop(2, 4, normed_grad_step, 0)

    def sibling_sum_step(z, carry):
        for x in range(2):
            to_sibling(z, x).wait_recv()
            mine = R[z, x, :, :, here.core].astype(F32) + SB[z, x].astype(F32)
            R[z, x, :, :, here.core] = mine.astype(BF16)
        return carry

    lax.fori_loop(0, 4, sibling_sum_step, 0)
    next(cotangents)
    sums_over_chips = scatter(here, copies, R, halves, wholes, GR)
    next(sums_over_chips)
    for _ in cotangents:
        pass

    spot = lax.broadcasted_iota(jnp.int32, (8, 128), 1)
    weights = jnp.where(spot == 0, 4096.0, jnp.where(spot == 1, 64.0, jnp.where(spot == 2, 1.0, 0.0)))
    token_row = dot(weights.astype(BF16), E[0, 1, :, :, :, :, 384:512].reshape(768, 128), NT)[0:1]
    token_row = token_row - ((here.dp * 8 + here.vocab) * 1024).astype(F32)

    def one_hot_step(m, carry):
        rows = pl.ds(pl.multiple_of(m * 256, 256), 256)
        entry = (lax.broadcasted_iota(jnp.int32, (256, 768), 0) + m * 256).astype(F32)
        OHT[rows, :] = jnp.where(entry == token_row, 1.0, 0.0).astype(BF16)
        return carry

    lax.fori_loop(0, 4, one_hot_step, 0)

    def table_unit(z, x):
        size = 512 - 128 * x
        at = z * 896 + x * 512

        def step(m, carry):
            rows = pl.ds(pl.multiple_of(m * 512, 512), 512)
            states = A[z, 1, :, :, :, :, 128 + 512 * x : 128 + 512 * x + size].reshape(768, size)
            cots = E[z, x, :, :, :, :, 0:size].reshape(768, size)
            block = dot(LGT[rows, :], states) + math.sqrt(width) * dot(OHT[rows, :], cots)
            HEAD[rows, at : at + size] = block.astype(BF16)
            return carry

        lax.fori_loop(0, 2, step, 0)

    stores = []
    for z in range(4):
        table_unit(z, 0)
        next(sums_over_chips)
        table_unit(z, 1)
        columns = pl.ds(z * 896, 896)
        stores.append(
            pltpu.make_async_copy(HEAD.at[:, columns], table_grad_hbm.at[:, columns], out_sems.at[z])
        )
        stores[-1].start()
    for _ in sums_over_chips:
        pass

    found = GR[...]
    normed_grad = jnp.where(low, found[:, :448], found[:, 64:])
    s_scale = SCALE[:, 0:1]
    normed = (sh * s_scale * sgain).astype(BF16).astype(F32)
    row = column_to_row(jnp.sum(normed_grad * normed, axis=1, keepdims=True))
    inner = row_to_column(vocab_sum(INNER, vocab_start(here, copies, INNER, row, row))[0:1])
    hidden_grad = s_scale * sgain * normed_grad - sh * s_scale * s_scale * inner / width
    hidden_grad_ref[...] = hidden_grad.astype(BF16)

    for copy in copies.all:
        copy.wait_send()

    def sibling_sent_step(z, carry):
        for x in range(2):
            to_sibling(z, x).wait_send()
        return carry

    lax.fori_loop(0, 4, sibling_sent_step, 0)
    for store in stores:
        store.wait()


def per_device(th, tgain, head, sh, sgain, table, ec, ids):
    halves, wholes = scatter_shapes()
    vmem, hbm = pl.BlockSpec(memory_space=pltpu.VMEM), pl.BlockSpec(memory_space=pl.ANY)
    return pl.pallas_call(
        kernel,
        out_shape=(jax.ShapeDtypeStruct(sh.shape, BF16), jax.ShapeDtypeStruct(table.shape, BF16)),
        in_specs=[vmem, vmem, hbm, vmem, vmem, hbm, vmem, vmem],
        out_specs=(vmem, hbm),
        scratch_shapes=[
            pltpu.VMEM((4, 2, 2, 4, 2, 48, 1024), BF16),
            pltpu.VMEM((4, 2, 2, 4, 2, 48, 512), BF16),
            pltpu.VMEM((4, 2, 2, 4, 2, 48, 512), BF16),
            pltpu.VMEM((4, 2, 2, 4, 48, 512), BF16),
            pltpu.VMEM(head.shape, BF16),
            pltpu.VMEM(table.shape, BF16),
            pltpu.VMEM((1024, 768), F32),
            pltpu.VMEM((1024, 768), F32),
            pltpu.VMEM((1024, 768), BF16),
            pltpu.VMEM((768, 1024), BF16),
            pltpu.VMEM((1024, 768), BF16),
            pltpu.VMEM((48, 512), F32),
            pltpu.VMEM((64, 512), BF16),
            pltpu.VMEM((64, 512), BF16),
            pltpu.VMEM((8, 8, 128), F32),
            pltpu.VMEM((8, 8, 128), F32),
            pltpu.VMEM((48, 128), F32),
            pltpu.VMEM((5, 8, 768), F32),
            pltpu.VMEM((10, 8, 768), F32),
            *halves,
            *wholes,
            pltpu.SemaphoreType.DMA((192,)),
            pltpu.SemaphoreType.DMA((192,)),
            pltpu.SemaphoreType.DMA((8,)),
            pltpu.SemaphoreType.DMA((8,)),
            pltpu.SemaphoreType.DMA((2,)),
            pltpu.SemaphoreType.DMA((4,)),
        ],
        compiler_params=pltpu.CompilerParams(
            collective_id=0, has_side_effects=True, vmem_limit_bytes=66 * 1024 * 1024 - 2 * 1024 * 1024
        ),
        name="distill",
    )(th, tgain[None, :], head, sh, sgain[None, :], table, ec, ids[:, None])


def solution(mesh):
    return jax.shard_map(
        per_device,
        mesh=mesh,
        in_specs=(
            P("dp", "vocab"),
            P("vocab"),
            P(("dp", "vocab"), None),
            P("dp", "vocab"),
            P("vocab"),
            P(("dp", "vocab"), None),
            P("dp", "vocab"),
            P("dp"),
        ),
        out_specs=(P("dp", "vocab"), P(("dp", "vocab"), None)),
        check_vma=False,
    )
```

time: 464 us -> 142 us (0.31)
  blocking collectives: 225 us -> 0 us
  Pallas kernels: 0 us -> 130 us
  waiting for transfers between devices: 123 us -> 0 us
  matrix products: 47.6 us -> 0 us
  other arithmetic: 41.8 us -> 0 us
  between operations: 15.9 us -> 0.64 us
    pallas_call x0 -> x1, Pallas kernels: none -> 130 us  [per_device(): pl.pallas_call(kernel, out_shape=(jax.ShapeDtypeStruct(sh.shape, BF16), j...]
    psum x1 -> x0, waiting for transfers between devices: 107 us -> none  [per_device(): lax.psum(jnp.dot(logit_grad, student_table, preferred_element_type=jnp.fl...]
    all_gather x3 -> x0, blocking collectives: 93 us -> none  [the longest x1 31.3 us: per_device(): lax.all_gather(teacher_hidden, 'vocab', axis=1, tiled=True)]
    psum x2 -> x0, blocking collectives: 85.4 us -> none  [the longest x1 67.6 us: per_device(): lax.psum((jnp.sum(t_exp, axis=1), jnp.sum(s_exp, axis=1)), ('dp', 'vocab'))]
    dot_general x4 -> x0, matrix products: 47.6 us -> none  [the longest x2 19.4 us: head_logits(): lax.dot_general(normed, table, (((1,), (1,)), ((), ())), preferred_elemen...]
    unnamed x2 -> x0, blocking collectives: 46.4 us -> none
    scatter-add x1 -> x0, other arithmetic: 28.4 us -> none  [per_device(): jax.ops.segment_sum(e_full.astype(jnp.float32) * math.sqrt(full_width), l...]
    all_gather x3 -> x0, waiting for transfers between devices: 15.9 us -> none  [the longest x1 15.9 us: per_device(): lax.all_gather(t_cols, 'dp', axis=0, tiled=True)]
  transfers between devices with their start and end apart: 4 -> 0, of which waited for: 2 -> 0; matrix products, arithmetic and copies ran while one was open for 20% -> 0% of each run, Pallas kernels for 0% -> 0%
where the time goes in v1:
time: 142 us
  Pallas kernels  130 us (92%)
  local copies, waits for them, and re-layouts  11.9 us (8%)
    pallas_call x1, Pallas kernels, per_device(): pl.pallas_call(kernel, out_shape=(jax.ShapeDtypeStruct(sh.shape, BF16), j...  130 us
    unnamed x2, local copies, waits for them, and re-layouts  8.02 us

profile of v1, /device:TPU:0, one launch (start us, length us, event | category | flops | bytes accessed | tf_op | source)
XLA Modules:
  0.0 142.1 jit_solution(10758654398216003841)
XLA Ops:
  0.6 1.3 broadcast_in_dim.10.sgain_ref
  1.9 1.3 broadcast_in_dim.9.tgain_ref
  3.2 1.3 copy.10.ids_ref
  4.5 129.6 %distill.1 = (bf16[48,448]{1,0:T(8,128)(2,1)}, bf16[1024,3584]{1,0:T(8,128)(2,1)}) custom-call(bf16[48,576]{1,0:T(8,128)(2,1)} %th_ref.1, bf16[1,576]{1,0:T(2,128)(2,1)} %broadcast_in_dim.9.tgain_ref, bf16[1024,4608]{1,0:T(8,128)(2,1)} %head_hbm.1, bf16[48,448]{1,0:T(8,128)(2,1)} %sh_ref.1, bf16[1,448]{1,0:T(2,128)(2,1)} %broadcast_in_dim.10.sgain_ref, ...), custom_call_target="tpu_custom_call" | custom-call | tf_op jit(solution)/shard_map/distill/pallas_call | solution.py:438
  134.1 1.4 %copy.13 = bf16[48,448]{1,0:T(8,128)(2,1)} copy(bf16[48,448]{1,0:T(8,128)(2,1)} %get-tuple-element.4) | data formatting | bytes 86016
  135.5 6.6 %copy.14 = bf16[1024,3584]{1,0:T(8,128)(2,1)} copy(bf16[1024,3584]{1,0:T(8,128)(2,1)} %get-tuple-element.5) | data formatting | bytes 14680064

commit v2 on v1

v2 whole, which is shorter than its diff:
```python
import math

import jax
import jax.numpy as jnp
from jax import lax
from jax.experimental import pallas as pl
from jax.experimental.pallas import tpu as pltpu
from jax.sharding import PartitionSpec as P

MESH = pl.DeviceIdType.MESH
F32, BF16 = jnp.float32, jnp.bfloat16
ORDER = (("z", "x", "y"), ("x", "y", "z"), ("y", "z", "x"))
PARTS = (1, 2, 0)
NT = (((1,), (1,)), ((), ()))
NN = (((1,), (0,)), ((), ()))


def dot(a, b, dims=NN):
    return lax.dot_general(a, b, dims, preferred_element_type=F32)


class Place:
    def __init__(self):
        dp, vocab = lax.axis_index("dp"), lax.axis_index("vocab")
        self.vocab, self.dp = vocab, dp
        self.core = dp % 2
        self.at = {"x": (dp // 8) * 2 + vocab % 2, "y": (dp // 2) % 4, "z": vocab // 2}
        self.x_lo = vocab % 2

    def device(self, core=None, **moved):
        at = {**self.at, **moved}
        core = self.core if core is None else core
        return ((at["x"] // 2) * 8 + at["y"] * 2 + core, at["z"] * 2 + at["x"] % 2)

    def along(self, axis, by):
        return (self.at[axis] + by) % 4

    def shifted(self, axis, by):
        return self.device(**{axis: self.along(axis, by)})

    def sibling(self):
        return self.device(core=1 - self.core)


class Copies:
    def __init__(self, send_sems, recv_sems):
        self.send_sems, self.recv_sems, self.count, self.all = send_sems, recv_sems, 0, []

    def start(self, src, dst, device):
        copy = pltpu.make_async_remote_copy(
            src_ref=src,
            dst_ref=dst,
            send_sem=self.send_sems.at[self.count],
            recv_sem=self.recv_sems.at[self.count],
            device_id=device,
            device_id_type=MESH,
        )
        self.count += 1
        copy.start()
        self.all.append(copy)
        return copy


def region(fixed, core, part, lanes):
    whole = slice(None)
    z, y = fixed.get("z", whole), fixed.get("y", whole)
    x_lo, x_hi = (fixed["x"] % 2, fixed["x"] // 2) if "x" in fixed else (whole, whole)
    return (z, x_lo, x_hi, y, core, pl.ds(16 * part, 16), lanes)


class Gather:
    def __init__(self, here, copies, buf, width):
        self.here, self.copies, self.buf, self.sibling = here, copies, buf, {}
        self.full, self.low, self.high = pl.ds(0, width), pl.ds(0, width // 2), pl.ds(width // 2, width // 2)

    def push(self, p, ph, by, lanes, device):
        here, axis = self.here, ORDER[p][ph]
        fixed = {a: here.at[a] for a in "xyz" if a not in ORDER[p][:ph]}
        fixed[axis] = here.along(axis, by)
        piece = self.buf.at[region(fixed, here.core, p, lanes)]
        return self.copies.start(piece, piece, device)

    def along(self, p, ph, by):
        return self.here.shifted(ORDER[p][ph], by)

    def to_sibling(self, p, by):
        self.sibling[p, by] = self.push(p, 2, by, self.full, self.here.sibling())

    def start_short(self, ph):
        self.short = [self.push(p, ph, 0, self.full, self.along(p, ph, by)) for by in (1, 3, 2) for p in PARTS]

    def wait_short(self):
        for copy in self.short:
            copy.wait_recv()

    def start_long(self):
        self.first = {}
        for right, left in ((self.low, self.high), (self.high, self.low)):
            for p in PARTS:
                self.first.setdefault((p, 1), []).append(self.push(p, 2, 0, right, self.along(p, 2, 1)))
                self.first.setdefault((p, -1), []).append(self.push(p, 2, 0, left, self.along(p, 2, -1)))
        for p in PARTS:
            self.to_sibling(p, 0)

    def forward_long(self):
        self.second = []
        for p in PARTS:
            self.first[p, 1][0].wait_recv()
            self.second.append(self.push(p, 2, -1, self.low, self.along(p, 2, 1)))
            self.first[p, -1][0].wait_recv()
            self.second.append(self.push(p, 2, 1, self.high, self.along(p, 2, -1)))

    def land_long(self):
        for p in PARTS:
            for by in (1, -1):
                self.first[p, by][1].wait_recv()
                self.to_sibling(p, -by)

    def finish_long(self):
        for p, right, left in zip(PARTS, self.second[::2], self.second[1::2]):
            right.wait_recv()
            left.wait_recv()
            self.to_sibling(p, 2)

    def wait_sibling(self, p, *moves):
        for by in moves or (0, -1, 1, 2):
            self.sibling[p, by].wait_recv()

    def steps(self):
        self.start_short(0)
        yield
        self.wait_short()
        self.start_short(1)
        yield
        self.wait_short()
        self.start_long()
        yield
        self.forward_long()
        yield
        self.land_long()
        yield
        self.finish_long()
        yield
        for p in PARTS:
            self.wait_sibling(p)


def scatter(here, copies, p, buf, half, whole, direct, result):
    low, high, full = pl.ds(0, 256), pl.ds(256, 256), pl.ds(0, 512)
    order = ORDER[p][::-1]

    def slab(ph, by, lanes):
        fixed = {a: here.at[a] for a in order[:ph]}
        fixed[order[ph]] = here.along(order[ph], by)
        return region(fixed, here.core, p, lanes)

    right, left = here.shifted(order[0], 1), here.shifted(order[0], -1)
    first = (
        copies.start(buf.at[slab(0, 2, low)], half.at[0], right),
        copies.start(buf.at[slab(0, 2, high)], half.at[1], left),
    )
    yield
    first[0].wait_recv()
    at = slab(0, 1, low)
    buf[at] = (buf[at].astype(F32) + half[0].astype(F32)).astype(BF16)
    second = [copies.start(buf.at[slab(0, 1, full)], whole.at[0], right)]
    first[1].wait_recv()
    at = slab(0, -1, high)
    buf[at] = (buf[at].astype(F32) + half[1].astype(F32)).astype(BF16)
    second.append(copies.start(buf.at[slab(0, -1, full)], whole.at[1], left))
    yield
    for copy in second:
        copy.wait_recv()
    at = slab(0, 0, full)
    buf[at] = (buf[at].astype(F32) + whole[0].astype(F32) + whole[1].astype(F32)).astype(BF16)
    for ph, got in zip((1, 2), direct):
        sent = [
            copies.start(buf.at[slab(ph, by, full)], got.at[by - 1], here.shifted(order[ph], by)) for by in (1, 3, 2)
        ]
        yield
        total = buf[slab(ph, 0, full)].astype(F32)
        for copy in sent:
            copy.wait_recv()
        for i in range(3):
            total = total + got[i].astype(F32)
        if ph == 1:
            buf[slab(ph, 0, full)] = total.astype(BF16)
        else:
            result[pl.ds(16 * p, 16), :] = total


def scatter_shapes():
    sizes = {"x": (2, 2), "y": (4,), "z": (4,)}
    shapes = []
    for order in ORDER:
        left = ["x", "y", "z"]
        for ph, axis in enumerate(order[::-1]):
            left.remove(axis)
            dims = sum((sizes[a] for a in ("z", "x", "y") if a in left), ())
            if ph == 0:
                shapes.append(pltpu.VMEM((2, *dims, 16, 256), BF16))
            shapes.append(pltpu.VMEM((2 if ph == 0 else 3, *dims, 16, 512), BF16))
    return shapes


def totals(here, copies, sent, got):
    groups = (
        [here.device(core=core, x=here.along("x", by)) for core, by in OTHERS(here.core)],
        [here.shifted("y", by) for by in (1, 2, 3)],
        [here.shifted("z", by) for by in (1, 2, 3)],
    )
    slot = 0
    for step, targets in enumerate(groups):
        started = [copies.start(sent.at[step], got.at[slot + i], target) for i, target in enumerate(targets)]
        yield
        total = sent[step]
        for i, copy in enumerate(started):
            copy.wait_recv()
            total = total + got[slot + i]
        slot += len(targets)
        sent[step + 1] = total


def OTHERS(core):
    return [(1 - core, 0)] + [(c, by) for by in (1, 2, 3) for c in (core, 1 - core)]


def column_to_row(column):
    rows, lanes = lax.broadcasted_iota(jnp.int32, (48, 128), 0), lax.broadcasted_iota(jnp.int32, (48, 128), 1)
    return jnp.sum(jnp.where(rows == lanes, column, 0.0), axis=0, keepdims=True)


def row_to_column(row):
    rows, lanes = lax.broadcasted_iota(jnp.int32, (48, 128), 0), lax.broadcasted_iota(jnp.int32, (48, 128), 1)
    return jnp.sum(jnp.where(rows == lanes, row, 0.0), axis=1, keepdims=True)


def vocab_start(here, copies, slots, first_row, second_row):
    rows = lax.broadcasted_iota(jnp.int32, (8, 128), 0)
    slots[here.vocab] = jnp.where(rows == 0, first_row, jnp.where(rows == 1, second_row, 0.0))
    mine = slots.at[here.vocab]
    return [copies.start(mine, mine, (here.dp, (here.vocab + by) % 8)) for by in range(1, 8)]


def vocab_sum(slots, started):
    for copy in started:
        copy.wait_recv()
    total = slots[0]
    for slot in range(1, 8):
        total = total + slots[slot]
    return total


def kernel(
    th_hbm, tgain_hbm, head_hbm, sh_hbm, sgain_hbm, table_hbm, ec_hbm, ids_hbm,
    hidden_grad_ref, table_grad_hbm,
    TH, TGAIN, SH, SGAIN, EC, IDS,
    A, E, R, SB, HEAD, ST, EXPT, STANH, LGT, LG, OHT, GR, MSG, GOT, SQ, INNER, SCALE, TS, TR,
    *rest,
):
    landing, (send_sems, recv_sems, sib_send, sib_recv, load_sems, out_sems) = rest[:12], rest[12:]
    here = Place()
    copies = Copies(send_sems, recv_sems)
    x_lo = here.x_lo
    width = 3584

    barrier = pltpu.get_barrier_semaphore()
    partners = [here.shifted(axis, by) for axis in "yz" for by in (1, 2, 3)]
    partners += [here.device(core=core, x=here.along("x", by)) for core, by in OTHERS(here.core)]
    partners += [(here.dp, here.along("z", by) * 2 + 1 - x_lo) for by in (1, 2, 3)]
    for partner in partners:
        pl.semaphore_signal(barrier, inc=1, device_id=partner, device_id_type=MESH)

    loads = [
        pltpu.make_async_copy(src, dst, load_sems.at[i])
        for i, (src, dst) in enumerate(
            [(th_hbm, TH), (sh_hbm, SH), (tgain_hbm, TGAIN), (sgain_hbm, SGAIN), (ec_hbm, EC), (ids_hbm, IDS),
             (head_hbm, HEAD), (table_hbm, ST)]
        )
    ]
    for load in loads:
        load.start()
    for load in loads[:6]:
        load.wait()

    th, sh, ec = TH[...].astype(F32), SH[...].astype(F32), EC[...].astype(F32)
    tgain, sgain = TGAIN[...].reshape(1, 576).astype(F32), SGAIN[...].reshape(1, 448).astype(F32)
    low = x_lo == 0
    t_part = jnp.sum(th * th, axis=1, keepdims=True)
    s_part = jnp.sum(sh * sh, axis=1, keepdims=True)
    MSG[0:48, :] = jnp.concatenate([jnp.where(low, sh, th[:, :448]), ec[:, :64]], axis=1).astype(BF16)
    gain_row = jnp.concatenate([jnp.where(low, sgain, tgain[:, :448]), jnp.zeros((1, 64), F32)], axis=1)
    MSG[48:64, :] = jnp.broadcast_to(gain_row, (16, 512)).astype(BF16)
    t_row, s_row = column_to_row(t_part), column_to_row(s_part)
    pl.semaphore_wait(barrier, len(partners))
    started = vocab_start(here, copies, SQ, t_row, s_row)
    pair = copies.start(MSG, GOT, (here.dp, here.vocab + 1 - 2 * x_lo))
    sums = vocab_sum(SQ, started)
    t_scale = lax.rsqrt(row_to_column(sums[0:1]) / 4608 + 1e-06)
    s_scale = lax.rsqrt(row_to_column(sums[1:2]) / width + 1e-06)
    SCALE[...] = jnp.broadcast_to(s_scale, (48, 128))
    pair.wait_recv()
    got = GOT[0:48, :].astype(F32)
    got_gain = GOT[48:64, :].astype(F32)[0:1]

    values = jnp.where(
        low,
        jnp.concatenate([th, got[:, :448]], axis=1),
        jnp.concatenate([th[:, 448:], got[:, :448], sh], axis=1),
    )
    gains = jnp.where(
        low,
        jnp.concatenate([tgain, got_gain[:, :448]], axis=1),
        jnp.concatenate([tgain[:, 448:], got_gain[:, :448], sgain], axis=1),
    )
    lanes = lax.broadcasted_iota(jnp.int32, (48, 1024), 1)
    scales = jnp.where(jnp.logical_or(low, lanes < 128), t_scale, s_scale)
    own = (here.at["z"], x_lo, here.at["x"] // 2, here.at["y"], here.core)
    A[own] = (values * scales * gains).astype(BF16)

    states = Gather(here, copies, A, 1024)
    states.start_short(0)

    ids_row = IDS[...].reshape(1, 48).astype(F32)
    ids = row_to_column(jnp.concatenate([ids_row, jnp.zeros((1, 80), F32)], axis=1))
    spot = lax.broadcasted_iota(jnp.int32, (48, 128), 1)
    top = jnp.floor(ids * (1.0 / 4096.0))
    mid = jnp.floor((ids - 4096.0 * top) * (1.0 / 64.0))
    digits = jnp.where(
        spot == 0, top, jnp.where(spot == 1, mid, jnp.where(spot == 2, ids - 4096.0 * top - 64.0 * mid, 0.0))
    )
    E[own] = jnp.where(
        low,
        jnp.concatenate([ec, got[:, 448:]], axis=1),
        jnp.concatenate([ec[:, 64:], digits], axis=1),
    ).astype(BF16)

    states.wait_short()
    states.start_short(1)
    states.wait_short()
    states.start_long()
    loads[6].wait()
    loads[7].wait()

    def part(ref, z, x, p, lo, hi):
        return ref[z, x, :, :, :, 16 * p : 16 * p + 16, lo:hi].reshape(256, hi - lo)

    def half_rows(m):
        return pl.ds(pl.multiple_of(m * 512, 512), 512)

    def squash(p, m, t_raw, s_raw):
        rows = half_rows(m)
        t_value, s_value = jnp.exp(30.0 * jnp.tanh(t_raw * (1.0 / 30.0))), jnp.tanh(s_raw * (1.0 / 30.0))
        EXPT[p, rows, :] = t_value
        STANH[p, rows, :] = s_value
        sums = jnp.where(
            lax.broadcasted_iota(jnp.int32, (8, 256), 0) == 0,
            jnp.sum(t_value, axis=0, keepdims=True),
            jnp.sum(jnp.exp(30.0 * s_value), axis=0, keepdims=True),
        )
        TS[p, 0] = sums if m == 0 else TS[p, 0] + sums

    def block_logits(by, m, last=False):
        z = here.along("z", by)
        rows = half_rows(m)
        t_at, s_at = pl.multiple_of(z * 1152, 128), pl.multiple_of(z * 896, 128)
        t_raw = dot(HEAD[rows, pl.ds(t_at, 1024)], part(A, z, 0, 1, 0, 1024), NT)
        t_raw += dot(HEAD[rows, pl.ds(t_at + 1024, 128)], part(A, z, 1, 1, 0, 128), NT)
        s_raw = dot(ST[rows, pl.ds(s_at, 896)], part(A, z, 1, 1, 128, 1024), NT)
        if by != 0:
            t_raw += EXPT[1, rows, :]
            s_raw += STANH[1, rows, :]
        if last:
            squash(1, m, t_raw, s_raw)
        else:
            EXPT[1, rows, :] = t_raw
            STANH[1, rows, :] = s_raw

    def low_logits(p, m):
        rows = half_rows(m)
        return sum(dot(HEAD[rows, z * 1152 : z * 1152 + 1024], part(A, z, 0, p, 0, 1024), NT) for z in range(4))

    def high_logits(p, m):
        rows = half_rows(m)
        t_raw = dot(
            jnp.concatenate([HEAD[rows, z * 1152 + 1024 : z * 1152 + 1152] for z in range(4)], axis=1),
            jnp.concatenate([part(A, z, 1, p, 0, 128) for z in range(4)], axis=1),
            NT,
        )
        s_raw = dot(
            jnp.concatenate([ST[rows, z * 896 + 768 : z * 896 + 896] for z in range(4)], axis=1),
            jnp.concatenate([part(A, z, 1, p, 896, 1024) for z in range(4)], axis=1),
            NT,
        )
        for z in range(4):
            s_raw += dot(ST[rows, z * 896 : z * 896 + 768], part(A, z, 1, p, 128, 896), NT)
        return t_raw, s_raw

    def part_logits(p, m):
        t_raw, s_raw = high_logits(p, m)
        squash(p, m, t_raw + low_logits(p, m), s_raw)

    def early_logits(p, m):
        rows = half_rows(m)

        @pl.when(low)
        def _():
            EXPT[p, rows, :], STANH[p, rows, :] = high_logits(p, m)

        @pl.when(jnp.logical_not(low))
        def _():
            EXPT[p, rows, :] = low_logits(p, m)

    def late_logits(p, m):
        rows = half_rows(m)

        @pl.when(low)
        def _():
            squash(p, m, EXPT[p, rows, :] + low_logits(p, m), STANH[p, rows, :])

        @pl.when(jnp.logical_not(low))
        def _():
            t_raw, s_raw = high_logits(p, m)
            squash(p, m, EXPT[p, rows, :] + t_raw, s_raw)

    def start_totals(p):
        steps = totals(here, copies, TS.at[p], TR.at[p])
        next(steps)
        return steps

    def finish(steps):
        for _ in steps:
            pass

    cotangents = Gather(here, copies, E, 512).steps()

    states.wait_sibling(1, 0)
    block_logits(0, 0)
    states.forward_long()
    block_logits(0, 1)
    states.land_long()
    states.wait_sibling(1, -1, 1)
    for m in range(2):
        block_logits(-1, m)
        block_logits(1, m)
    states.wait_sibling(2, -1, 1)
    early_logits(2, 0)
    states.finish_long()
    next(cotangents)
    early_logits(2, 1)
    states.wait_sibling(1, 2)
    block_logits(2, 0, True)
    block_logits(2, 1, True)
    totals_of = {1: start_totals(1)}
    states.wait_sibling(2, 0, 2)
    late_logits(2, 0)
    next(cotangents)
    late_logits(2, 1)
    next(totals_of[1])
    totals_of[2] = start_totals(2)
    states.wait_sibling(0)
    part_logits(0, 0)
    next(cotangents)
    next(totals_of[1])
    next(totals_of[2])
    part_logits(0, 1)
    totals_of[0] = start_totals(0)
    next(cotangents)
    finish(totals_of[1])

    def gradient(p):
        inverse = 1.0 / TS[p, 3]
        t_inverse, s_inverse = inverse[0:1], inverse[1:2]

        def step(m, carry):
            rows = pl.ds(pl.multiple_of(m * 256, 256), 256)
            tanh = STANH[p, rows, :]
            grad = (jnp.exp(30.0 * tanh) * s_inverse - EXPT[p, rows, :] * t_inverse) * (1.0 - tanh * tanh)
            LGT[p, rows, :] = grad.astype(BF16)
            LG[p, :, rows] = grad.T.astype(BF16)
            return carry

        lax.fori_loop(0, 4, step, 0)

    def to_sibling(p, z):
        mine = pl.ds(16 * p, 16)
        return pltpu.make_async_remote_copy(
            src_ref=R.at[z, :, :, :, 1 - here.core, mine],
            dst_ref=SB.at[z, :, :, :, mine],
            send_sem=sib_send.at[p * 4 + z],
            recv_sem=sib_recv.at[p * 4 + z],
            device_id=here.sibling(),
            device_id_type=MESH,
        )

    def normed_grad(p, start, stop):
        def step(z, carry):
            for x in range(2):
                for half in range(2):
                    columns = pl.ds(pl.multiple_of(z * 896 + x * 384 + half * 256, 128), 256)
                    found = dot(LG[p], ST[:, columns]).astype(BF16)
                    R[z, x, :, :, :, 16 * p : 16 * p + 16, half * 256 : half * 256 + 256] = found.reshape(
                        2, 4, 2, 16, 256
                    )
            to_sibling(p, z).start()
            return carry

        lax.fori_loop(start, stop, step, 0)

    def start_scatter(p):
        def step(z, carry):
            to_sibling(p, z).wait_recv()
            at = (z, slice(None), slice(None), slice(None), here.core, pl.ds(16 * p, 16))
            mine = R[at].astype(F32) + SB[z, :, :, :, 16 * p : 16 * p + 16].astype(F32)
            R[at] = mine.astype(BF16)
            return carry

        lax.fori_loop(0, 4, step, 0)
        steps = scatter(
            here, copies, p, R, landing[4 * p], landing[4 * p + 1], landing[4 * p + 2 : 4 * p + 4], GR
        )
        next(steps)
        return steps

    gradient(1)
    normed_grad(1, 0, 2)
    next(totals_of[2])
    next(totals_of[0])
    next(cotangents)
    normed_grad(1, 2, 4)
    finish(totals_of[2])
    scatters = {1: start_scatter(1)}
    gradient(2)
    normed_grad(2, 0, 2)
    next(totals_of[0])
    next(cotangents)
    normed_grad(2, 2, 4)
    scatters[2] = start_scatter(2)
    finish(totals_of[0])
    gradient(0)
    normed_grad(0, 0, 2)
    next(scatters[1])
    normed_grad(0, 2, 4)
    scatters[0] = start_scatter(0)
    finish(cotangents)

    spot = lax.broadcasted_iota(jnp.int32, (8, 128), 1)
    weights = jnp.where(spot == 0, 4096.0, jnp.where(spot == 1, 64.0, jnp.where(spot == 2, 1.0, 0.0)))
    first_entry = ((here.dp * 8 + here.vocab) * 1024).astype(F32)

    def one_hot(p):
        token_row = dot(weights.astype(BF16), part(E, 0, 1, p, 384, 512), NT)[0:1] - first_entry

        def step(m, carry):
            rows = pl.ds(pl.multiple_of(m * 256, 256), 256)
            entry = (lax.broadcasted_iota(jnp.int32, (256, 256), 0) + m * 256).astype(F32)
            OHT[p, rows, :] = jnp.where(entry == token_row, 1.0, 0.0).astype(BF16)
            return carry

        lax.fori_loop(0, 4, step, 0)

    for p in PARTS:
        one_hot(p)

    def table_unit(z, x):
        size = 512 - 128 * x
        at = z * 896 + x * 512

        def step(m, carry):
            rows = half_rows(m)
            grads = jnp.concatenate([LGT[p, rows, :] for p in range(3)], axis=1)
            hot = jnp.concatenate([OHT[p, rows, :] for p in range(3)], axis=1)
            normed = jnp.concatenate(
                [part(A, z, 1, p, 128 + 512 * x, 128 + 512 * x + size) for p in range(3)], axis=0
            )
            cots = jnp.concatenate([part(E, z, x, p, 0, size) for p in range(3)], axis=0)
            found = dot(grads, normed) + math.sqrt(width) * dot(hot, cots)
            HEAD[rows, at : at + size] = found.astype(BF16)
            return carry

        lax.fori_loop(0, 2, step, 0)

    polls = {0: (2,), 2: (0,), 3: (1,), 5: (2, 1), 6: (2,), 7: (0,)}
    stores = []
    for unit in range(8):
        z = unit // 2
        table_unit(z, unit % 2)
        if unit % 2:
            columns = pl.ds(z * 896, 896)
            stores.append(
                pltpu.make_async_copy(HEAD.at[:, columns], table_grad_hbm.at[:, columns], out_sems.at[z])
            )
            stores[-1].start()
        for p in polls.get(unit, ()):
            next(scatters[p])
    next(scatters[0])
    for p in (1, 2, 0):
        finish(scatters[p])

    found = GR[...]
    normed_grad = jnp.where(low, found[:, :448], found[:, 64:])
    s_scale = SCALE[:, 0:1]
    normed = (sh * s_scale * sgain).astype(BF16).astype(F32)
    row = column_to_row(jnp.sum(normed_grad * normed, axis=1, keepdims=True))
    inner = row_to_column(vocab_sum(INNER, vocab_start(here, copies, INNER, row, row))[0:1])
    hidden_grad = s_scale * sgain * normed_grad - sh * s_scale * s_scale * inner / width
    hidden_grad_ref[...] = hidden_grad.astype(BF16)

    for copy in copies.all:
        copy.wait_send()
    for p in PARTS:
        for z in range(4):
            to_sibling(p, z).wait_send()
    for store in stores:
        store.wait()


def per_device(th, tgain, head, sh, sgain, table, ec, ids):
    vmem, hbm = pl.BlockSpec(memory_space=pltpu.VMEM), pl.BlockSpec(memory_space=pl.ANY)
    return pl.pallas_call(
        kernel,
        out_shape=(jax.ShapeDtypeStruct(sh.shape, BF16), jax.ShapeDtypeStruct(table.shape, BF16)),
        in_specs=[hbm] * 8,
        out_specs=(vmem, hbm),
        scratch_shapes=[
            *(pltpu.VMEM(small.shape, small.dtype) for small in (th, tgain, sh, sgain, ec, ids)),
            pltpu.VMEM((4, 2, 2, 4, 2, 48, 1024), BF16),
            pltpu.VMEM((4, 2, 2, 4, 2, 48, 512), BF16),
            pltpu.VMEM((4, 2, 2, 4, 2, 48, 512), BF16),
            pltpu.VMEM((4, 2, 2, 4, 48, 512), BF16),
            pltpu.VMEM(head.shape, BF16),
            pltpu.VMEM(table.shape, BF16),
            pltpu.VMEM((3, 1024, 256), F32),
            pltpu.VMEM((3, 1024, 256), F32),
            pltpu.VMEM((3, 1024, 256), BF16),
            pltpu.VMEM((3, 256, 1024), BF16),
            pltpu.VMEM((3, 1024, 256), BF16),
            pltpu.VMEM((48, 512), F32),
            pltpu.VMEM((64, 512), BF16),
            pltpu.VMEM((64, 512), BF16),
            pltpu.VMEM((8, 8, 128), F32),
            pltpu.VMEM((8, 8, 128), F32),
            pltpu.VMEM((48, 128), F32),
            pltpu.VMEM((3, 4, 8, 256), F32),
            pltpu.VMEM((3, 13, 8, 256), F32),
            *scatter_shapes(),
            pltpu.SemaphoreType.DMA((256,)),
            pltpu.SemaphoreType.DMA((256,)),
            pltpu.SemaphoreType.DMA((12,)),
            pltpu.SemaphoreType.DMA((12,)),
            pltpu.SemaphoreType.DMA((8,)),
            pltpu.SemaphoreType.DMA((4,)),
        ],
        compiler_params=pltpu.CompilerParams(
            collective_id=0, has_side_effects=True, vmem_limit_bytes=66 * 1024 * 1024 - 2 * 1024 * 1024
        ),
        name="distill",
    )(th, tgain, head, sh, sgain, table, ec, ids)


def solution(mesh):
    return jax.shard_map(
        per_device,
        mesh=mesh,
        in_specs=(
            P("dp", "vocab"),
            P("vocab"),
            P(("dp", "vocab"), None),
            P("dp", "vocab"),
            P("vocab"),
            P(("dp", "vocab"), None),
            P("dp", "vocab"),
            P("dp"),
        ),
        out_specs=(P("dp", "vocab"), P(("dp", "vocab"), None)),
        check_vma=False,
    )
```

time: 142 us -> 129 us (0.908)
  Pallas kernels: 130 us -> 120 us
  local copies, waits for them, and re-layouts: 11.9 us -> 8.02 us
    pallas_call x1, Pallas kernels: 130 us -> 120 us  [per_device(): pl.pallas_call(kernel, out_shape=(jax.ShapeDtypeStruct(sh.shape, BF16), j...]
    broadcast_in_dim x3 -> x0, local copies, waits for them, and re-layouts: 3.87 us -> none  [the longest x1 1.35 us: per_device(): ids[:, None]]
where the time goes in v2:
time: 129 us
  Pallas kernels  120 us (93%)
  local copies, waits for them, and re-layouts  8.02 us (6%)
    pallas_call x1, Pallas kernels, per_device(): pl.pallas_call(kernel, out_shape=(jax.ShapeDtypeStruct(sh.shape, BF16), j...  120 us
    unnamed x2, local copies, waits for them, and re-layouts  8.02 us

profile of v2, /device:TPU:0, one launch (start us, length us, event | category | flops | bytes accessed | tf_op | source)
XLA Modules:
  0.0 129.0 jit_solution(5204546000683899155)
XLA Ops:
  0.6 120.4 %distill.1 = (bf16[48,448]{1,0:T(8,128)(2,1)}, bf16[1024,3584]{1,0:T(8,128)(2,1)}) custom-call(bf16[48,576]{1,0:T(8,128)(2,1)} %th_hbm.1, bf16[576]{0:T(1024)(128)(2,1)} %tgain_hbm.1, bf16[1024,4608]{1,0:T(8,128)(2,1)} %head_hbm.1, bf16[48,448]{1,0:T(8,128)(2,1)} %sh_hbm.1, bf16[448]{0:T(512)(128)(2,1)} %sgain_hbm.1, bf16[1024,3584]{1,0:T(8,128)(2,1)} %table_hbm.1, ...), custom_call_target="tpu_custom_call" | custom-call | tf_op jit(solution)/shard_map/distill/pallas_call | solution.py:620
  121.0 1.4 %copy.12 = bf16[48,448]{1,0:T(8,128)(2,1)} copy(bf16[48,448]{1,0:T(8,128)(2,1)} %get-tuple-element.4) | data formatting | bytes 86016
  122.4 6.6 %copy.13 = bf16[1024,3584]{1,0:T(8,128)(2,1)} copy(bf16[1024,3584]{1,0:T(8,128)(2,1)} %get-tuple-element.5) | data formatting | bytes 14680064

commit v3 on v2

--- a/solution.py
+++ b/solution.py
@@ -11,6 +11,7 @@
 F32, BF16 = jnp.float32, jnp.bfloat16
 ORDER = (("z", "x", "y"), ("x", "y", "z"), ("y", "z", "x"))
 PARTS = (1, 2, 0)
+SENDS, RECEIVES = 64, 174
 NT = (((1,), (1,)), ((), ()))
 NN = (((1,), (0,)), ((), ()))
 
@@ -44,21 +45,28 @@
 
 class Copies:
     def __init__(self, send_sems, recv_sems):
-        self.send_sems, self.recv_sems, self.count, self.all = send_sems, recv_sems, 0, []
+        self.send_sems, self.recv_sems, self.all = send_sems, recv_sems, []
 
     def start(self, src, dst, device):
+        count = len(self.all)
+        if count >= SENDS:
+            self.all[count - SENDS].wait_send()
         copy = pltpu.make_async_remote_copy(
             src_ref=src,
             dst_ref=dst,
-            send_sem=self.send_sems.at[self.count],
-            recv_sem=self.recv_sems.at[self.count],
+            send_sem=self.send_sems.at[count % SENDS],
+            recv_sem=self.recv_sems.at[count],
             device_id=device,
             device_id_type=MESH,
         )
-        self.count += 1
         copy.start()
         self.all.append(copy)
         return copy
+
+    def finish(self):
+        assert len(self.all) == RECEIVES, len(self.all)
+        for copy in self.all[-SENDS:]:
+            copy.wait_send()
 
 
 def region(fixed, core, part, lanes):
@@ -94,27 +102,22 @@
             copy.wait_recv()
 
     def start_long(self):
-        self.first = {}
-        for right, left in ((self.low, self.high), (self.high, self.low)):
-            for p in PARTS:
-                self.first.setdefault((p, 1), []).append(self.push(p, 2, 0, right, self.along(p, 2, 1)))
-                self.first.setdefault((p, -1), []).append(self.push(p, 2, 0, left, self.along(p, 2, -1)))
+        self.first = {
+            (p, by): self.push(p, 2, 0, self.full, self.along(p, 2, by)) for p in PARTS for by in (1, -1)
+        }
         for p in PARTS:
             self.to_sibling(p, 0)
 
     def forward_long(self):
         self.second = []
         for p in PARTS:
-            self.first[p, 1][0].wait_recv()
+            self.first[p, 1].wait_recv()
             self.second.append(self.push(p, 2, -1, self.low, self.along(p, 2, 1)))
-            self.first[p, -1][0].wait_recv()
+            self.first[p, -1].wait_recv()
             self.second.append(self.push(p, 2, 1, self.high, self.along(p, 2, -1)))
-
-    def land_long(self):
         for p in PARTS:
-            for by in (1, -1):
-                self.first[p, by][1].wait_recv()
-                self.to_sibling(p, -by)
+            for by in (-1, 1):
+                self.to_sibling(p, by)
 
     def finish_long(self):
         for p, right, left in zip(PARTS, self.second[::2], self.second[1::2]):
@@ -125,24 +128,6 @@
     def wait_sibling(self, p, *moves):
         for by in moves or (0, -1, 1, 2):
             self.sibling[p, by].wait_recv()
-
-    def steps(self):
-        self.start_short(0)
-        yield
-        self.wait_short()
-        self.start_short(1)
-        yield
-        self.wait_short()
-        self.start_long()
-        yield
-        self.forward_long()
-        yield
-        self.land_long()
-        yield
-        self.finish_long()
-        yield
-        for p in PARTS:
-            self.wait_sibling(p)
 
 
 def scatter(here, copies, p, buf, half, whole, direct, result):
@@ -255,7 +240,7 @@
     th_hbm, tgain_hbm, head_hbm, sh_hbm, sgain_hbm, table_hbm, ec_hbm, ids_hbm,
     hidden_grad_ref, table_grad_hbm,
     TH, TGAIN, SH, SGAIN, EC, IDS,
-    A, E, R, SB, HEAD, ST, EXPT, STANH, LGT, LG, OHT, GR, MSG, GOT, SQ, INNER, SCALE, TS, TR,
+    A, E, R, SB, HEAD, ST, EXPT, SRAW, LGT, LG, OHT, GR, MSG, GOT, SQ, SCALE, TS, TR, TI, TIR,
     *rest,
 ):
     landing, (send_sems, recv_sems, sib_send, sib_recv, load_sems, out_sems) = rest[:12], rest[12:]
@@ -335,10 +320,15 @@
         jnp.concatenate([ec[:, 64:], digits], axis=1),
     ).astype(BF16)
 
+    cotangents = Gather(here, copies, E, 512)
+    cotangents.start_short(0)
     states.wait_short()
     states.start_short(1)
+    cotangents.wait_short()
+    cotangents.start_short(1)
     states.wait_short()
     states.start_long()
+    cotangents.wait_short()
     loads[6].wait()
     loads[7].wait()
 
@@ -350,13 +340,14 @@
 
     def squash(p, m, t_raw, s_raw):
         rows = half_rows(m)
-        t_value, s_value = jnp.exp(30.0 * jnp.tanh(t_raw * (1.0 / 30.0))), jnp.tanh(s_raw * (1.0 / 30.0))
+        t_value = jnp.exp(30.0 * jnp.tanh(t_raw * (1.0 / 30.0)))
+        s_value = jnp.exp(30.0 * jnp.tanh(s_raw * (1.0 / 30.0)))
         EXPT[p, rows, :] = t_value
-        STANH[p, rows, :] = s_value
+        SRAW[p, rows, :] = s_raw
         sums = jnp.where(
             lax.broadcasted_iota(jnp.int32, (8, 256), 0) == 0,
             jnp.sum(t_value, axis=0, keepdims=True),
-            jnp.sum(jnp.exp(30.0 * s_value), axis=0, keepdims=True),
+            jnp.sum(s_value, axis=0, keepdims=True),
         )
         TS[p, 0] = sums if m == 0 else TS[p, 0] + sums
 
@@ -369,12 +360,12 @@
         s_raw = dot(ST[rows, pl.ds(s_at, 896)], part(A, z, 1, 1, 128, 1024), NT)
         if by != 0:
             t_raw += EXPT[1, rows, :]
-            s_raw += STANH[1, rows, :]
+            s_raw += SRAW[1, rows, :]
         if last:
             squash(1, m, t_raw, s_raw)
         else:
             EXPT[1, rows, :] = t_raw
-            STANH[1, rows, :] = s_raw
+            SRAW[1, rows, :] = s_raw
 
     def low_logits(p, m):
         rows = half_rows(m)
@@ -405,7 +396,7 @@
 
         @pl.when(low)
         def _():
-            EXPT[p, rows, :], STANH[p, rows, :] = high_logits(p, m)
+            EXPT[p, rows, :], SRAW[p, rows, :] = high_logits(p, m)
 
         @pl.when(jnp.logical_not(low))
         def _():
@@ -416,7 +407,7 @@
 
         @pl.when(low)
         def _():
-            squash(p, m, EXPT[p, rows, :] + low_logits(p, m), STANH[p, rows, :])
+            squash(p, m, EXPT[p, rows, :] + low_logits(p, m), SRAW[p, rows, :])
 
         @pl.when(jnp.logical_not(low))
         def _():
@@ -432,55 +423,53 @@
         for _ in steps:
             pass
 
-    cotangents = Gather(here, copies, E, 512).steps()
-
     states.wait_sibling(1, 0)
-    block_logits(0, 0)
+    for m in range(2):
+        block_logits(0, m)
     states.forward_long()
-    block_logits(0, 1)
-    states.land_long()
     states.wait_sibling(1, -1, 1)
     for m in range(2):
         block_logits(-1, m)
         block_logits(1, m)
     states.wait_sibling(2, -1, 1)
     early_logits(2, 0)
+    early_logits(2, 1)
     states.finish_long()
-    next(cotangents)
-    early_logits(2, 1)
+    cotangents.start_long()
     states.wait_sibling(1, 2)
     block_logits(2, 0, True)
     block_logits(2, 1, True)
     totals_of = {1: start_totals(1)}
     states.wait_sibling(2, 0, 2)
     late_logits(2, 0)
-    next(cotangents)
     late_logits(2, 1)
+    cotangents.forward_long()
     next(totals_of[1])
     totals_of[2] = start_totals(2)
     states.wait_sibling(0)
     part_logits(0, 0)
-    next(cotangents)
     next(totals_of[1])
     next(totals_of[2])
     part_logits(0, 1)
     totals_of[0] = start_totals(0)
-    next(cotangents)
     finish(totals_of[1])
+    cotangents.finish_long()
 
     def gradient(p):
         inverse = 1.0 / TS[p, 3]
         t_inverse, s_inverse = inverse[0:1], inverse[1:2]
 
-        def step(m, carry):
+        def step(m, total):
             rows = pl.ds(pl.multiple_of(m * 256, 256), 256)
-            tanh = STANH[p, rows, :]
+            raw = SRAW[p, rows, :]
+            tanh = jnp.tanh(raw * (1.0 / 30.0))
             grad = (jnp.exp(30.0 * tanh) * s_inverse - EXPT[p, rows, :] * t_inverse) * (1.0 - tanh * tanh)
-            LGT[p, rows, :] = grad.astype(BF16)
+            rounded = grad.astype(BF16)
+            LGT[p, rows, :] = rounded
             LG[p, :, rows] = grad.T.astype(BF16)
-            return carry
-
-        lax.fori_loop(0, 4, step, 0)
+            return total + jnp.sum(rounded.astype(F32) * raw, axis=0, keepdims=True)
+
+        return lax.fori_loop(0, 4, step, jnp.zeros((1, 256), F32))
 
     def to_sibling(p, z):
         mine = pl.ds(16 * p, 16)
@@ -522,27 +511,33 @@
         next(steps)
         return steps
 
-    gradient(1)
+    inner_parts = {1: gradient(1)}
     normed_grad(1, 0, 2)
     next(totals_of[2])
     next(totals_of[0])
-    next(cotangents)
     normed_grad(1, 2, 4)
     finish(totals_of[2])
     scatters = {1: start_scatter(1)}
-    gradient(2)
+    inner_parts[2] = gradient(2)
     normed_grad(2, 0, 2)
     next(totals_of[0])
-    next(cotangents)
     normed_grad(2, 2, 4)
     scatters[2] = start_scatter(2)
     finish(totals_of[0])
-    gradient(0)
+    inner_parts[0] = gradient(0)
+
+    which = lax.broadcasted_iota(jnp.int32, (8, 256), 0)
+    TI[0] = jnp.where(which == 0, inner_parts[0], jnp.where(which == 1, inner_parts[1], inner_parts[2]))
+    inner_steps = totals(here, copies, TI, TIR)
+    next(inner_steps)
     normed_grad(0, 0, 2)
     next(scatters[1])
+    next(inner_steps)
     normed_grad(0, 2, 4)
     scatters[0] = start_scatter(0)
-    finish(cotangents)
+    next(inner_steps)
+    for p in PARTS:
+        cotangents.wait_sibling(p)
 
     spot = lax.broadcasted_iota(jnp.int32, (8, 128), 1)
     weights = jnp.where(spot == 0, 4096.0, jnp.where(spot == 1, 64.0, jnp.where(spot == 2, 1.0, 0.0)))
@@ -580,7 +575,7 @@
 
         lax.fori_loop(0, 2, step, 0)
 
-    polls = {0: (2,), 2: (0,), 3: (1,), 5: (2, 1), 6: (2,), 7: (0,)}
+    polls = {0: (2,), 1: (0,), 3: (1,), 4: (1, 2), 5: (0, 2), 6: (0,)}
     stores = []
     for unit in range(8):
         z = unit // 2
@@ -593,21 +588,25 @@
             stores[-1].start()
         for p in polls.get(unit, ()):
             next(scatters[p])
-    next(scatters[0])
+    finish(inner_steps)
     for p in (1, 2, 0):
         finish(scatters[p])
 
     found = GR[...]
-    normed_grad = jnp.where(low, found[:, :448], found[:, 64:])
+    own_grad = jnp.where(low, found[:, :448], found[:, 64:])
     s_scale = SCALE[:, 0:1]
-    normed = (sh * s_scale * sgain).astype(BF16).astype(F32)
-    row = column_to_row(jnp.sum(normed_grad * normed, axis=1, keepdims=True))
-    inner = row_to_column(vocab_sum(INNER, vocab_start(here, copies, INNER, row, row))[0:1])
-    hidden_grad = s_scale * sgain * normed_grad - sh * s_scale * s_scale * inner / width
+    lane = lax.broadcasted_iota(jnp.int32, (16, 256), 1) - lax.broadcasted_iota(jnp.int32, (16, 256), 0)
+    inner = jnp.concatenate(
+        [
+            jnp.sum(jnp.where(lane == here.dp * 16, TI[3, p : p + 1, :], 0.0), axis=1, keepdims=True)
+            for p in range(3)
+        ],
+        axis=0,
+    )
+    hidden_grad = s_scale * sgain * own_grad - sh * s_scale * s_scale * inner / width
     hidden_grad_ref[...] = hidden_grad.astype(BF16)
 
-    for copy in copies.all:
-        copy.wait_send()
+    copies.finish()
     for p in PARTS:
         for z in range(4):
             to_sibling(p, z).wait_send()
@@ -615,9 +614,24 @@
         store.wait()
 
 
+def place_results(hidden_from, table_from, hidden_to, table_to, small, large, in_sems, out_sems):
+    rows = table_from.shape[0] // 4
+    pieces = [(table_from.at[at], large.at[at], table_to.at[at]) for at in (pl.ds(i * rows, rows) for i in range(4))]
+    pieces.append((hidden_from, small, hidden_to))
+    ins = [pltpu.make_async_copy(a, b, in_sems.at[i]) for i, (a, b, _) in enumerate(pieces)]
+    outs = [pltpu.make_async_copy(b, c, out_sems.at[i]) for i, (_, b, c) in enumerate(pieces)]
+    for copy in ins:
+        copy.start()
+    for copy, out in zip(ins, outs):
+        copy.wait()
+        out.start()
+    for out in outs:
+        out.wait()
+
+
 def per_device(th, tgain, head, sh, sgain, table, ec, ids):
     vmem, hbm = pl.BlockSpec(memory_space=pltpu.VMEM), pl.BlockSpec(memory_space=pl.ANY)
-    return pl.pallas_call(
+    found = pl.pallas_call(
         kernel,
         out_shape=(jax.ShapeDtypeStruct(sh.shape, BF16), jax.ShapeDtypeStruct(table.shape, BF16)),
         in_specs=[hbm] * 8,
@@ -639,13 +653,14 @@
             pltpu.VMEM((64, 512), BF16),
             pltpu.VMEM((64, 512), BF16),
             pltpu.VMEM((8, 8, 128), F32),
-            pltpu.VMEM((8, 8, 128), F32),
             pltpu.VMEM((48, 128), F32),
             pltpu.VMEM((3, 4, 8, 256), F32),
             pltpu.VMEM((3, 13, 8, 256), F32),
+            pltpu.VMEM((4, 8, 256), F32),
+            pltpu.VMEM((13, 8, 256), F32),
             *scatter_shapes(),
-            pltpu.SemaphoreType.DMA((256,)),
-            pltpu.SemaphoreType.DMA((256,)),
+            pltpu.SemaphoreType.DMA((SENDS,)),
+            pltpu.SemaphoreType.DMA((RECEIVES,)),
             pltpu.SemaphoreType.DMA((12,)),
             pltpu.SemaphoreType.DMA((12,)),
             pltpu.SemaphoreType.DMA((8,)),
@@ -656,6 +671,20 @@
         ),
         name="distill",
     )(th, tgain, head, sh, sgain, table, ec, ids)
+    return pl.pallas_call(
+        place_results,
+        out_shape=tuple(jax.ShapeDtypeStruct(a.shape, a.dtype) for a in found),
+        in_specs=[hbm] * 2,
+        out_specs=(hbm, hbm),
+        scratch_shapes=[
+            pltpu.VMEM(sh.shape, BF16),
+            pltpu.VMEM(table.shape, BF16),
+            pltpu.SemaphoreType.DMA((5,)),
+            pltpu.SemaphoreType.DMA((5,)),
+        ],
+        compiler_params=pltpu.CompilerParams(vmem_limit_bytes=64 * 1024 * 1024),
+        name="place",
+    )(*found)
 
 
 def solution(mesh):

time: 129 us -> 120 us (0.930)
  local copies, waits for them, and re-layouts: 8.02 us -> 0 us
    unnamed x2 -> x0, local copies, waits for them, and re-layouts: 8.02 us -> none
    pallas_call x1, Pallas kernels: 120 us -> 113 us  [per_device(): pl.pallas_call(kernel, out_shape=(jax.ShapeDtypeStruct(sh.shape, BF16), j...]
    pallas_call x0 -> x1, Pallas kernels: none -> 6.1 us  [per_device(): pl.pallas_call(place_results, out_shape=tuple((jax.ShapeDtypeStruct(a.sha...]
where the time goes in v3:
time: 120 us; the launch traced here: 119 us
  Pallas kernels  119 us (99%)
    pallas_call x1, Pallas kernels, per_device(): pl.pallas_call(kernel, out_shape=(jax.ShapeDtypeStruct(sh.shape, BF16), j...  113 us
    pallas_call x1, Pallas kernels, per_device(): pl.pallas_call(place_results, out_shape=tuple((jax.ShapeDtypeStruct(a.sha...  6.1 us

profile of v3, /device:TPU:0, one launch (start us, length us, event | category | flops | bytes accessed | tf_op | source)
XLA Modules:
  0.0 119.4 jit_solution(902647032892042049)
XLA Ops:
  0.6 112.5 %distill.1 = (bf16[48,448]{1,0:T(8,128)(2,1)}, bf16[1024,3584]{1,0:T(8,128)(2,1)}) custom-call(bf16[48,576]{1,0:T(8,128)(2,1)} %th_hbm.1, bf16[576]{0:T(1024)(128)(2,1)} %tgain_hbm.1, bf16[1024,4608]{1,0:T(8,128)(2,1)} %head_hbm.1, bf16[48,448]{1,0:T(8,128)(2,1)} %sh_hbm.1, bf16[448]{0:T(512)(128)(2,1)} %sgain_hbm.1, bf16[1024,3584]{1,0:T(8,128)(2,1)} %table_hbm.1, ...), custom_call_target="tpu_custom_call" | custom-call | tf_op jit(solution)/shard_map/distill/pallas_call | solution.py:634
  113.2 6.1 %place.1 = (bf16[48,448]{1,0:T(8,128)(2,1)}, bf16[1024,3584]{1,0:T(8,128)(2,1)}) custom-call(bf16[48,448]{1,0:T(8,128)(2,1)} %get-tuple-element.4.hidden_from, bf16[1024,3584]{1,0:T(8,128)(2,1)} %get-tuple-element.5.table_from), custom_call_target="tpu_custom_call" | custom-call | tf_op jit(solution)/shard_map/place/pallas_call | solution.py:674

commit v4 on v3

--- a/solution.py
+++ b/solution.py
@@ -11,7 +11,7 @@
 F32, BF16 = jnp.float32, jnp.bfloat16
 ORDER = (("z", "x", "y"), ("x", "y", "z"), ("y", "z", "x"))
 PARTS = (1, 2, 0)
-SENDS, RECEIVES = 64, 174
+SENDS, RECEIVES = 64, 181
 NT = (((1,), (1,)), ((), ()))
 NN = (((1,), (0,)), ((), ()))
 
@@ -108,6 +108,17 @@
         for p in PARTS:
             self.to_sibling(p, 0)
 
+    def start_direct(self):
+        self.first = {
+            (p, by): self.push(p, 2, 0, self.full, self.along(p, 2, by)) for by in (1, -1, 2) for p in PARTS
+        }
+
+    def finish_direct(self):
+        for p in PARTS:
+            for by in (1, -1, 2):
+                self.first[p, by].wait_recv()
+                self.to_sibling(p, -by if by != 2 else 2)
+
     def forward_long(self):
         self.second = []
         for p in PARTS:
@@ -130,9 +141,17 @@
             self.sibling[p, by].wait_recv()
 
 
-def scatter(here, copies, p, buf, half, whole, direct, result):
-    low, high, full = pl.ds(0, 256), pl.ds(256, 256), pl.ds(0, 512)
-    order = ORDER[p][::-1]
+SCATTERS = {
+    "1": (1, ("z", "y", "x"), 0, 512),
+    "2": (2, ("x", "z", "y"), 0, 512),
+    "0a": (0, ("y", "x", "z"), 0, 256),
+    "0b": (0, ("z", "x", "y"), 256, 256),
+}
+
+
+def scatter(here, copies, p, order, start, width, buf, landing, result):
+    half, whole, *direct = landing
+    low, high, full = pl.ds(start, width // 2), pl.ds(start + width // 2, width // 2), pl.ds(start, width)
 
     def slab(ph, by, lanes):
         fixed = {a: here.at[a] for a in order[:ph]}
@@ -171,20 +190,18 @@
         if ph == 1:
             buf[slab(ph, 0, full)] = total.astype(BF16)
         else:
-            result[pl.ds(16 * p, 16), :] = total
+            result[pl.ds(16 * p, 16), full] = total
 
 
 def scatter_shapes():
     sizes = {"x": (2, 2), "y": (4,), "z": (4,)}
     shapes = []
-    for order in ORDER:
-        left = ["x", "y", "z"]
-        for ph, axis in enumerate(order[::-1]):
-            left.remove(axis)
-            dims = sum((sizes[a] for a in ("z", "x", "y") if a in left), ())
+    for _, order, _, width in SCATTERS.values():
+        for ph in range(3):
+            dims = sum((sizes[a] for a in ("z", "x", "y") if a in order[ph + 1 :]), ())
             if ph == 0:
-                shapes.append(pltpu.VMEM((2, *dims, 16, 256), BF16))
-            shapes.append(pltpu.VMEM((2 if ph == 0 else 3, *dims, 16, 512), BF16))
+                shapes.append(pltpu.VMEM((2, *dims, 16, width // 2), BF16))
+            shapes.append(pltpu.VMEM((2 if ph == 0 else 3, *dims, 16, width), BF16))
     return shapes
 
 
@@ -238,12 +255,12 @@
 
 def kernel(
     th_hbm, tgain_hbm, head_hbm, sh_hbm, sgain_hbm, table_hbm, ec_hbm, ids_hbm,
-    hidden_grad_ref, table_grad_hbm,
+    hidden_grad_ref, HEAD,
     TH, TGAIN, SH, SGAIN, EC, IDS,
-    A, E, R, SB, HEAD, ST, EXPT, SRAW, LGT, LG, OHT, GR, MSG, GOT, SQ, SCALE, TS, TR, TI, TIR,
+    A, E, R, SB, ST, EXPT, SRAW, LGT, LG, OHT, GR, MSG, GOT, SQ, SCALE, TS, TR, TI, TIR,
     *rest,
 ):
-    landing, (send_sems, recv_sems, sib_send, sib_recv, load_sems, out_sems) = rest[:12], rest[12:]
+    landing, (send_sems, recv_sems, sib_send, sib_recv, load_sems) = rest[:16], rest[16:]
     here = Place()
     copies = Copies(send_sems, recv_sems)
     x_lo = here.x_lo
@@ -435,7 +452,7 @@
     early_logits(2, 0)
     early_logits(2, 1)
     states.finish_long()
-    cotangents.start_long()
+    cotangents.start_direct()
     states.wait_sibling(1, 2)
     block_logits(2, 0, True)
     block_logits(2, 1, True)
@@ -443,17 +460,18 @@
     states.wait_sibling(2, 0, 2)
     late_logits(2, 0)
     late_logits(2, 1)
-    cotangents.forward_long()
     next(totals_of[1])
     totals_of[2] = start_totals(2)
     states.wait_sibling(0)
     part_logits(0, 0)
+    for p in PARTS:
+        cotangents.to_sibling(p, 0)
     next(totals_of[1])
     next(totals_of[2])
     part_logits(0, 1)
     totals_of[0] = start_totals(0)
     finish(totals_of[1])
-    cotangents.finish_long()
+    cotangents.finish_direct()
 
     def gradient(p):
         inverse = 1.0 / TS[p, 3]
@@ -486,30 +504,69 @@
         def step(z, carry):
             for x in range(2):
                 for half in range(2):
-                    columns = pl.ds(pl.multiple_of(z * 896 + x * 384 + half * 256, 128), 256)
-                    found = dot(LG[p], ST[:, columns]).astype(BF16)
-                    R[z, x, :, :, :, 16 * p : 16 * p + 16, half * 256 : half * 256 + 256] = found.reshape(
-                        2, 4, 2, 16, 256
-                    )
+                    normed_block(p, z, x, half)
             to_sibling(p, z).start()
             return carry
 
         lax.fori_loop(start, stop, step, 0)
+
+    def normed_block(p, z, x, half):
+        columns = pl.ds(pl.multiple_of(z * 896 + x * 384 + half * 256, 128), 256)
+        found = dot(LG[p], ST[:, columns]).astype(BF16)
+        R[z, x, :, :, :, 16 * p : 16 * p + 16, half * 256 : half * 256 + 256] = found.reshape(2, 4, 2, 16, 256)
+
+    def half_to_sibling(half, pair):
+        at, mine, lanes = pl.ds(2 * pair, 2), pl.ds(0, 16), pl.ds(256 * half, 256)
+        return pltpu.make_async_remote_copy(
+            src_ref=R.at[at, :, :, :, 1 - here.core, mine, lanes],
+            dst_ref=SB.at[at, :, :, :, mine, lanes],
+            send_sem=sib_send.at[half * 2 + pair],
+            recv_sem=sib_recv.at[half * 2 + pair],
+            device_id=here.sibling(),
+            device_id_type=MESH,
+        )
+
+    def normed_grad_half(half):
+        for pair in range(2):
+
+            def step(z, carry):
+                for x in range(2):
+                    normed_block(0, z, x, half)
+                return carry
+
+            lax.fori_loop(2 * pair, 2 * pair + 2, step, 0)
+            half_to_sibling(half, pair).start()
+
+    def add_sibling(p, z, lanes):
+        at = (z, slice(None), slice(None), slice(None), here.core, pl.ds(16 * p, 16), lanes)
+        mine = R[at].astype(F32) + SB[z, :, :, :, 16 * p : 16 * p + 16, lanes].astype(F32)
+        R[at] = mine.astype(BF16)
+
+    def start_steps(name):
+        i = 4 * list(SCATTERS).index(name)
+        steps = scatter(here, copies, *SCATTERS[name], R, landing[i : i + 4], GR)
+        next(steps)
+        return steps
 
     def start_scatter(p):
         def step(z, carry):
             to_sibling(p, z).wait_recv()
-            at = (z, slice(None), slice(None), slice(None), here.core, pl.ds(16 * p, 16))
-            mine = R[at].astype(F32) + SB[z, :, :, :, 16 * p : 16 * p + 16].astype(F32)
-            R[at] = mine.astype(BF16)
+            add_sibling(p, z, pl.ds(0, 512))
             return carry
 
         lax.fori_loop(0, 4, step, 0)
-        steps = scatter(
-            here, copies, p, R, landing[4 * p], landing[4 * p + 1], landing[4 * p + 2 : 4 * p + 4], GR
-        )
-        next(steps)
-        return steps
+        return start_steps(str(p))
+
+    def start_scatter_half(half):
+        for pair in range(2):
+            half_to_sibling(half, pair).wait_recv()
+
+            def step(z, carry):
+                add_sibling(0, z, pl.ds(256 * half, 256))
+                return carry
+
+            lax.fori_loop(2 * pair, 2 * pair + 2, step, 0)
+        return start_steps("0ab"[0] + "ab"[half])
 
     inner_parts = {1: gradient(1)}
     normed_grad(1, 0, 2)
@@ -530,12 +587,14 @@
     TI[0] = jnp.where(which == 0, inner_parts[0], jnp.where(which == 1, inner_parts[1], inner_parts[2]))
     inner_steps = totals(here, copies, TI, TIR)
     next(inner_steps)
-    normed_grad(0, 0, 2)
+    normed_grad_half(0)
     next(scatters[1])
     next(inner_steps)
-    normed_grad(0, 2, 4)
-    scatters[0] = start_scatter(0)
+    scatters["a"] = start_scatter_half(0)
+    normed_grad_half(1)
+    scatters["b"] = start_scatter_half(1)
     next(inner_steps)
+    next(scatters[2])
     for p in PARTS:
         cotangents.wait_sibling(p)
 
@@ -575,22 +634,14 @@
 
         lax.fori_loop(0, 2, step, 0)
 
-    polls = {0: (2,), 1: (0,), 3: (1,), 4: (1, 2), 5: (0, 2), 6: (0,)}
-    stores = []
+    polls = {0: ("a",), 1: ("b",), 2: (1,), 3: ("a", 1), 4: ("b", 2), 5: (2,), 6: ("a",), 7: ("b",)}
     for unit in range(8):
-        z = unit // 2
-        table_unit(z, unit % 2)
-        if unit % 2:
-            columns = pl.ds(z * 896, 896)
-            stores.append(
-                pltpu.make_async_copy(HEAD.at[:, columns], table_grad_hbm.at[:, columns], out_sems.at[z])
-            )
-            stores[-1].start()
+        table_unit(unit // 2, unit % 2)
         for p in polls.get(unit, ()):
             next(scatters[p])
     finish(inner_steps)
-    for p in (1, 2, 0):
-        finish(scatters[p])
+    for name in (1, 2, "a", "b"):
+        finish(scatters[name])
 
     found = GR[...]
     own_grad = jnp.where(low, found[:, :448], found[:, 64:])
@@ -607,23 +658,21 @@
     hidden_grad_ref[...] = hidden_grad.astype(BF16)
 
     copies.finish()
-    for p in PARTS:
+    for p in (1, 2):
         for z in range(4):
             to_sibling(p, z).wait_send()
-    for store in stores:
-        store.wait()
-
-
-def place_results(hidden_from, table_from, hidden_to, table_to, small, large, in_sems, out_sems):
+    for half in range(2):
+        for pair in range(2):
+            half_to_sibling(half, pair).wait_send()
+
+
+def place_results(hidden_from, table_from, hidden_to, table_to, out_sems):
     rows = table_from.shape[0] // 4
-    pieces = [(table_from.at[at], large.at[at], table_to.at[at]) for at in (pl.ds(i * rows, rows) for i in range(4))]
-    pieces.append((hidden_from, small, hidden_to))
-    ins = [pltpu.make_async_copy(a, b, in_sems.at[i]) for i, (a, b, _) in enumerate(pieces)]
-    outs = [pltpu.make_async_copy(b, c, out_sems.at[i]) for i, (_, b, c) in enumerate(pieces)]
-    for copy in ins:
-        copy.start()
-    for copy, out in zip(ins, outs):
-        copy.wait()
+    columns = pl.ds(0, table_to.shape[1])
+    pieces = [(table_from.at[at, columns], table_to.at[at]) for at in (pl.ds(i * rows, rows) for i in range(4))]
+    pieces.append((hidden_from, hidden_to))
+    outs = [pltpu.make_async_copy(a, b, out_sems.at[i]) for i, (a, b) in enumerate(pieces)]
+    for out in outs:
         out.start()
     for out in outs:
         out.wait()
@@ -633,16 +682,15 @@
     vmem, hbm = pl.BlockSpec(memory_space=pltpu.VMEM), pl.BlockSpec(memory_space=pl.ANY)
     found = pl.pallas_call(
         kernel,
-        out_shape=(jax.ShapeDtypeStruct(sh.shape, BF16), jax.ShapeDtypeStruct(table.shape, BF16)),
+        out_shape=(pltpu.VMEM(sh.shape, BF16), pltpu.VMEM(head.shape, BF16)),
         in_specs=[hbm] * 8,
-        out_specs=(vmem, hbm),
+        out_specs=(vmem, vmem),
         scratch_shapes=[
             *(pltpu.VMEM(small.shape, small.dtype) for small in (th, tgain, sh, sgain, ec, ids)),
             pltpu.VMEM((4, 2, 2, 4, 2, 48, 1024), BF16),
             pltpu.VMEM((4, 2, 2, 4, 2, 48, 512), BF16),
             pltpu.VMEM((4, 2, 2, 4, 2, 48, 512), BF16),
             pltpu.VMEM((4, 2, 2, 4, 48, 512), BF16),
-            pltpu.VMEM(head.shape, BF16),
             pltpu.VMEM(table.shape, BF16),
             pltpu.VMEM((3, 1024, 256), F32),
             pltpu.VMEM((3, 1024, 256), F32),
@@ -664,25 +712,19 @@
             pltpu.SemaphoreType.DMA((12,)),
             pltpu.SemaphoreType.DMA((12,)),
             pltpu.SemaphoreType.DMA((8,)),
-            pltpu.SemaphoreType.DMA((4,)),
         ],
         compiler_params=pltpu.CompilerParams(
-            collective_id=0, has_side_effects=True, vmem_limit_bytes=66 * 1024 * 1024 - 2 * 1024 * 1024
+            collective_id=0, has_side_effects=True, vmem_limit_bytes=54 * 1024 * 1024
         ),
         name="distill",
     )(th, tgain, head, sh, sgain, table, ec, ids)
     return pl.pallas_call(
         place_results,
-        out_shape=tuple(jax.ShapeDtypeStruct(a.shape, a.dtype) for a in found),
-        in_specs=[hbm] * 2,
+        out_shape=(jax.ShapeDtypeStruct(sh.shape, BF16), jax.ShapeDtypeStruct(table.shape, BF16)),
+        in_specs=[vmem, vmem],
         out_specs=(hbm, hbm),
-        scratch_shapes=[
-            pltpu.VMEM(sh.shape, BF16),
-            pltpu.VMEM(table.shape, BF16),
-            pltpu.SemaphoreType.DMA((5,)),
-            pltpu.SemaphoreType.DMA((5,)),
-        ],
-        compiler_params=pltpu.CompilerParams(vmem_limit_bytes=64 * 1024 * 1024),
+        scratch_shapes=[pltpu.SemaphoreType.DMA((5,))],
+        compiler_params=pltpu.CompilerParams(vmem_limit_bytes=32 * 1024 * 1024),
         name="place",
     )(*found)
 

time: 120 us -> 121 us (level)
    pallas_call x2, Pallas kernels: 119 us -> 120 us  [the longest x1 117 us: per_device(): pl.pallas_call(kernel, out_shape=(pltpu.VMEM(sh.shape, BF16), pltpu.VMEM(...]
where the time goes in v4:
time: 121 us
  Pallas kernels  120 us (99%)
    pallas_call x1, Pallas kernels, per_device(): pl.pallas_call(kernel, out_shape=(pltpu.VMEM(sh.shape, BF16), pltpu.VMEM(...  117 us
    pallas_call x1, Pallas kernels, per_device(): pl.pallas_call(place_results, out_shape=(jax.ShapeDtypeStruct(sh.shape, B...  3.09 us

profile of v4, /device:TPU:0, one launch (start us, length us, event | category | flops | bytes accessed | tf_op | source)
XLA Modules:
  0.0 120.7 jit_solution(2016351312556833562)
XLA Ops:
  0.6 116.8 %distill.1 = (bf16[48,448]{1,0:T(8,128)(2,1)S(1)}, bf16[1024,4608]{1,0:T(8,128)(2,1)S(1)}) custom-call(bf16[48,576]{1,0:T(8,128)(2,1)} %th_hbm.1, bf16[576]{0:T(1024)(128)(2,1)} %tgain_hbm.1, bf16[1024,4608]{1,0:T(8,128)(2,1)} %head_hbm.1, bf16[48,448]{1,0:T(8,128)(2,1)} %sh_hbm.1, bf16[448]{0:T(512)(128)(2,1)} %sgain_hbm.1, bf16[1024,3584]{1,0:T(8,128)(2,1)} %table_hbm.1, ...), custom_call_target="tpu_custom_call" | custom-call | tf_op jit(solution)/shard_map/distill/pallas_call | solution.py:683
  117.4 3.1 %place.1 = (bf16[48,448]{1,0:T(8,128)(2,1)}, bf16[1024,3584]{1,0:T(8,128)(2,1)}) custom-call(bf16[48,448]{1,0:T(8,128)(2,1)S(1)} %get-tuple-element.4.hidden_from, bf16[1024,4608]{1,0:T(8,128)(2,1)S(1)} %get-tuple-element.5.table_from), custom_call_target="tpu_custom_call" | custom-call | tf_op jit(solution)/shard_map/place/pallas_call | solution.py:721

commit v5 on v3

--- a/solution.py
+++ b/solution.py
@@ -101,12 +101,13 @@
         for copy in self.short:
             copy.wait_recv()
 
-    def start_long(self):
+    def start_long(self, sibling=True):
         self.first = {
             (p, by): self.push(p, 2, 0, self.full, self.along(p, 2, by)) for p in PARTS for by in (1, -1)
         }
-        for p in PARTS:
-            self.to_sibling(p, 0)
+        if sibling:
+            for p in PARTS:
+                self.to_sibling(p, 0)
 
     def forward_long(self):
         self.second = []
@@ -238,12 +239,12 @@
 
 def kernel(
     th_hbm, tgain_hbm, head_hbm, sh_hbm, sgain_hbm, table_hbm, ec_hbm, ids_hbm,
-    hidden_grad_ref, table_grad_hbm,
+    hidden_grad_ref, HEAD,
     TH, TGAIN, SH, SGAIN, EC, IDS,
-    A, E, R, SB, HEAD, ST, EXPT, SRAW, LGT, LG, OHT, GR, MSG, GOT, SQ, SCALE, TS, TR, TI, TIR,
+    A, E, R, SB, ST, EXPT, SRAW, LGT, LG, OHT, GR, MSG, GOT, SQ, SCALE, TS, TR, TI, TIR,
     *rest,
 ):
-    landing, (send_sems, recv_sems, sib_send, sib_recv, load_sems, out_sems) = rest[:12], rest[12:]
+    landing, (send_sems, recv_sems, sib_send, sib_recv, load_sems) = rest[:12], rest[12:]
     here = Place()
     copies = Copies(send_sems, recv_sems)
     x_lo = here.x_lo
@@ -435,7 +436,7 @@
     early_logits(2, 0)
     early_logits(2, 1)
     states.finish_long()
-    cotangents.start_long()
+    cotangents.start_long(sibling=False)
     states.wait_sibling(1, 2)
     block_logits(2, 0, True)
     block_logits(2, 1, True)
@@ -443,6 +444,8 @@
     states.wait_sibling(2, 0, 2)
     late_logits(2, 0)
     late_logits(2, 1)
+    for p in PARTS:
+        cotangents.to_sibling(p, 0)
     cotangents.forward_long()
     next(totals_of[1])
     totals_of[2] = start_totals(2)
@@ -576,16 +579,8 @@
         lax.fori_loop(0, 2, step, 0)
 
     polls = {0: (2,), 1: (0,), 3: (1,), 4: (1, 2), 5: (0, 2), 6: (0,)}
-    stores = []
     for unit in range(8):
-        z = unit // 2
-        table_unit(z, unit % 2)
-        if unit % 2:
-            columns = pl.ds(z * 896, 896)
-            stores.append(
-                pltpu.make_async_copy(HEAD.at[:, columns], table_grad_hbm.at[:, columns], out_sems.at[z])
-            )
-            stores[-1].start()
+        table_unit(unit // 2, unit % 2)
         for p in polls.get(unit, ()):
             next(scatters[p])
     finish(inner_steps)
@@ -610,20 +605,15 @@
     for p in PARTS:
         for z in range(4):
             to_sibling(p, z).wait_send()
-    for store in stores:
-        store.wait()
-
-
-def place_results(hidden_from, table_from, hidden_to, table_to, small, large, in_sems, out_sems):
+
+
+def place_results(hidden_from, table_from, hidden_to, table_to, out_sems):
     rows = table_from.shape[0] // 4
-    pieces = [(table_from.at[at], large.at[at], table_to.at[at]) for at in (pl.ds(i * rows, rows) for i in range(4))]
-    pieces.append((hidden_from, small, hidden_to))
-    ins = [pltpu.make_async_copy(a, b, in_sems.at[i]) for i, (a, b, _) in enumerate(pieces)]
-    outs = [pltpu.make_async_copy(b, c, out_sems.at[i]) for i, (_, b, c) in enumerate(pieces)]
-    for copy in ins:
-        copy.start()
-    for copy, out in zip(ins, outs):
-        copy.wait()
+    columns = pl.ds(0, table_to.shape[1])
+    pieces = [(table_from.at[at, columns], table_to.at[at]) for at in (pl.ds(i * rows, rows) for i in range(4))]
+    pieces.append((hidden_from, hidden_to))
+    outs = [pltpu.make_async_copy(a, b, out_sems.at[i]) for i, (a, b) in enumerate(pieces)]
+    for out in outs:
         out.start()
     for out in outs:
         out.wait()
@@ -633,16 +623,15 @@
     vmem, hbm = pl.BlockSpec(memory_space=pltpu.VMEM), pl.BlockSpec(memory_space=pl.ANY)
     found = pl.pallas_call(
         kernel,
-        out_shape=(jax.ShapeDtypeStruct(sh.shape, BF16), jax.ShapeDtypeStruct(table.shape, BF16)),
+        out_shape=(pltpu.VMEM(sh.shape, BF16), pltpu.VMEM(head.shape, BF16)),
         in_specs=[hbm] * 8,
-        out_specs=(vmem, hbm),
+        out_specs=(vmem, vmem),
         scratch_shapes=[
             *(pltpu.VMEM(small.shape, small.dtype) for small in (th, tgain, sh, sgain, ec, ids)),
             pltpu.VMEM((4, 2, 2, 4, 2, 48, 1024), BF16),
             pltpu.VMEM((4, 2, 2, 4, 2, 48, 512), BF16),
             pltpu.VMEM((4, 2, 2, 4, 2, 48, 512), BF16),
             pltpu.VMEM((4, 2, 2, 4, 48, 512), BF16),
-            pltpu.VMEM(head.shape, BF16),
             pltpu.VMEM(table.shape, BF16),
             pltpu.VMEM((3, 1024, 256), F32),
             pltpu.VMEM((3, 1024, 256), F32),
@@ -664,25 +653,19 @@
             pltpu.SemaphoreType.DMA((12,)),
             pltpu.SemaphoreType.DMA((12,)),
             pltpu.SemaphoreType.DMA((8,)),
-            pltpu.SemaphoreType.DMA((4,)),
         ],
         compiler_params=pltpu.CompilerParams(
-            collective_id=0, has_side_effects=True, vmem_limit_bytes=66 * 1024 * 1024 - 2 * 1024 * 1024
+            collective_id=0, has_side_effects=True, vmem_limit_bytes=54 * 1024 * 1024
         ),
         name="distill",
     )(th, tgain, head, sh, sgain, table, ec, ids)
     return pl.pallas_call(
         place_results,
-        out_shape=tuple(jax.ShapeDtypeStruct(a.shape, a.dtype) for a in found),
-        in_specs=[hbm] * 2,
+        out_shape=(jax.ShapeDtypeStruct(sh.shape, BF16), jax.ShapeDtypeStruct(table.shape, BF16)),
+        in_specs=[vmem, vmem],
         out_specs=(hbm, hbm),
-        scratch_shapes=[
-            pltpu.VMEM(sh.shape, BF16),
-            pltpu.VMEM(table.shape, BF16),
-            pltpu.SemaphoreType.DMA((5,)),
-            pltpu.SemaphoreType.DMA((5,)),
-        ],
-        compiler_params=pltpu.CompilerParams(vmem_limit_bytes=64 * 1024 * 1024),
+        scratch_shapes=[pltpu.SemaphoreType.DMA((5,))],
+        compiler_params=pltpu.CompilerParams(vmem_limit_bytes=32 * 1024 * 1024),
         name="place",
     )(*found)
 

time: 120 us -> 116 us (0.967)
  Pallas kernels: 119 us -> 115 us
    pallas_call x2, Pallas kernels: 119 us -> 115 us  [the longest x1 112 us: per_device(): pl.pallas_call(kernel, out_shape=(pltpu.VMEM(sh.shape, BF16), pltpu.VMEM(...]
where the time goes in v5:
time: 116 us
  Pallas kernels  115 us (99%)
    pallas_call x1, Pallas kernels, per_device(): pl.pallas_call(kernel, out_shape=(pltpu.VMEM(sh.shape, BF16), pltpu.VMEM(...  112 us
    pallas_call x1, Pallas kernels, per_device(): pl.pallas_call(place_results, out_shape=(jax.ShapeDtypeStruct(sh.shape, B...  3.09 us

profile of v5, /device:TPU:0, one launch (start us, length us, event | category | flops | bytes accessed | tf_op | source)
XLA Modules:
  0.0 115.8 jit_solution(15419048048605112824)
XLA Ops:
  0.6 111.9 %distill.1 = (bf16[48,448]{1,0:T(8,128)(2,1)S(1)}, bf16[1024,4608]{1,0:T(8,128)(2,1)S(1)}) custom-call(bf16[48,576]{1,0:T(8,128)(2,1)} %th_hbm.1, bf16[576]{0:T(1024)(128)(2,1)} %tgain_hbm.1, bf16[1024,4608]{1,0:T(8,128)(2,1)} %head_hbm.1, bf16[48,448]{1,0:T(8,128)(2,1)} %sh_hbm.1, bf16[448]{0:T(512)(128)(2,1)} %sgain_hbm.1, bf16[1024,3584]{1,0:T(8,128)(2,1)} %table_hbm.1, ...), custom_call_target="tpu_custom_call" | custom-call | tf_op jit(solution)/shard_map/distill/pallas_call | solution.py:624
  112.5 3.1 %place.1 = (bf16[48,448]{1,0:T(8,128)(2,1)}, bf16[1024,3584]{1,0:T(8,128)(2,1)}) custom-call(bf16[48,448]{1,0:T(8,128)(2,1)S(1)} %get-tuple-element.4.hidden_from, bf16[1024,4608]{1,0:T(8,128)(2,1)S(1)} %get-tuple-element.5.table_from), custom_call_target="tpu_custom_call" | custom-call | tf_op jit(solution)/shard_map/place/pallas_call | solution.py:662

commit v6 on v5

--- a/solution.py
+++ b/solution.py
@@ -515,12 +515,11 @@
         return steps
 
     inner_parts = {1: gradient(1)}
-    normed_grad(1, 0, 2)
     next(totals_of[2])
+    normed_grad(1, 0, 4)
     next(totals_of[0])
-    normed_grad(1, 2, 4)
+    scatters = {1: start_scatter(1)}
     finish(totals_of[2])
-    scatters = {1: start_scatter(1)}
     inner_parts[2] = gradient(2)
     normed_grad(2, 0, 2)
     next(totals_of[0])
@@ -533,12 +532,11 @@
     TI[0] = jnp.where(which == 0, inner_parts[0], jnp.where(which == 1, inner_parts[1], inner_parts[2]))
     inner_steps = totals(here, copies, TI, TIR)
     next(inner_steps)
-    normed_grad(0, 0, 2)
+    normed_grad(0, 0, 4)
+    scatters[0] = start_scatter(0)
     next(scatters[1])
     next(inner_steps)
-    normed_grad(0, 2, 4)
-    scatters[0] = start_scatter(0)
-    next(inner_steps)
+    scatters["inner"] = inner_steps
     for p in PARTS:
         cotangents.wait_sibling(p)
 
@@ -578,7 +576,7 @@
 
         lax.fori_loop(0, 2, step, 0)
 
-    polls = {0: (2,), 1: (0,), 3: (1,), 4: (1, 2), 5: (0, 2), 6: (0,)}
+    polls = {0: (2,), 1: (0, "inner"), 3: (1,), 4: (1, 2), 5: (0, 2), 6: (0,)}
     for unit in range(8):
         table_unit(unit // 2, unit % 2)
         for p in polls.get(unit, ()):

time: 116 us -> 113 us (0.974)
  Pallas kernels: 115 us -> 112 us
    pallas_call x1, Pallas kernels: 112 us -> 109 us  [per_device(): pl.pallas_call(kernel, out_shape=(pltpu.VMEM(sh.shape, BF16), pltpu.VMEM(...]
where the time goes in v6:
time: 113 us; the launch traced here: 112 us
  Pallas kernels  112 us (99%)
    pallas_call x1, Pallas kernels, per_device(): pl.pallas_call(kernel, out_shape=(pltpu.VMEM(sh.shape, BF16), pltpu.VMEM(...  109 us
    pallas_call x1, Pallas kernels, per_device(): pl.pallas_call(place_results, out_shape=(jax.ShapeDtypeStruct(sh.shape, B...  3.09 us

profile of v6, /device:TPU:0, one launch (start us, length us, event | category | flops | bytes accessed | tf_op | source)
XLA Modules:
  0.0 112.4 jit_solution(11098476581381492960)
XLA Ops:
  0.6 108.6 %distill.1 = (bf16[48,448]{1,0:T(8,128)(2,1)S(1)}, bf16[1024,4608]{1,0:T(8,128)(2,1)S(1)}) custom-call(bf16[48,576]{1,0:T(8,128)(2,1)} %th_hbm.1, bf16[576]{0:T(1024)(128)(2,1)} %tgain_hbm.1, bf16[1024,4608]{1,0:T(8,128)(2,1)} %head_hbm.1, bf16[48,448]{1,0:T(8,128)(2,1)} %sh_hbm.1, bf16[448]{0:T(512)(128)(2,1)} %sgain_hbm.1, bf16[1024,3584]{1,0:T(8,128)(2,1)} %table_hbm.1, ...), custom_call_target="tpu_custom_call" | custom-call | tf_op jit(solution)/shard_map/distill/pallas_call | solution.py:622
  109.2 3.1 %place.1 = (bf16[48,448]{1,0:T(8,128)(2,1)}, bf16[1024,3584]{1,0:T(8,128)(2,1)}) custom-call(bf16[48,448]{1,0:T(8,128)(2,1)S(1)} %get-tuple-element.4.hidden_from, bf16[1024,4608]{1,0:T(8,128)(2,1)S(1)} %get-tuple-element.5.table_from), custom_call_target="tpu_custom_call" | custom-call | tf_op jit(solution)/shard_map/place/pallas_call | solution.py:660
